TPU v7x, 512 devices: a whole 4x4x16 slice. The times are simulated.
512 devices in a mesh: slide: 16 (over z), ctx: 32 (over y, x, core).
Axes of the slice: x: 4, y: 4, z: 16, core: 2. Of those that a mesh axis runs over, the one named last changes fastest.
Arguments:
- tiles: bfloat16 [16, 16384, 768], P('slide', 'ctx'), may hold values from -40 to 40
- tile_pos: int32 [16, 16384], P('slide', 'ctx'), may hold values from 0 to 16383, as said below
- lengths: int32 [16], P('slide'), may hold values from 4096 to 16384, as said below
- qkv_weight: bfloat16 [768, 1152], replicated, may hold values from -0.21875 to 0.21875
- out_weight: bfloat16 [384, 768], replicated, may hold values from -0.3125 to 0.3125
- cotangent: bfloat16 [16, 16384, 768], P('slide', 'ctx'), may hold values from -6 to 6
Outputs:
- tile_grads: bfloat16 [16, 16384, 768], P('slide', 'ctx')
- out_weight_grad: float32 [294912], P(('slide', 'ctx'))
- far_kv_grads: float32 [16, 2, 6, 1024, 64], P('slide', None, None, 'ctx')
Inputs may be any that keep to these rules, and one draw needn't show every extreme that they name: `tile_pos`: for every slide the entries are a permutation of its 16384 positions; the 512 entries held by one device of ctx contain exactly 16 positions of each block of 512 consecutive positions, in no particular order. `lengths`: at least one slide has all 16384 positions live.
All inputs are finite; a program needn't handle non-finite values.
Results may differ from a plain program's by a relative error of at most 0.014.
The roundings to bfloat16 on the way count: a program that leaves them out, or rounds other values in their place, can miss the bound.
Values may be sent and summed in bfloat16 or wider, within the bound.
No kernel may reach another device: no remote copies, remote signals or barrier semaphores. Data moves between devices by JAX's collectives and lax.ppermute only.
A program may use at most 128 MiB of HBM per device.

v0:
```python
import math

import jax
import jax.numpy as jnp
from jax import lax
from jax.sharding import PartitionSpec as P

HD = 64
WIDE_RATE2 = 16


NEGATIVE_FLOOR = -1e30


def dilate(tensor, stride):
    number = tensor.shape[1]
    lattice = tensor.reshape(tensor.shape[0] // stride, stride, number, tensor.shape[2])
    return jnp.stack([lattice[:, offset, offset, :] for offset in range(number)], 0)


def selector(number, stride):
    return jnp.arange(stride)[None, :] == jnp.arange(number)[:, None]


def spread(values, stride, filler):
    chosen = selector(values.shape[0], stride)
    return jnp.where(chosen[:, None, :], values[:, :, None], filler).reshape(values.shape[0], -1)


def spread_rows(values, stride):
    chosen = selector(values.shape[0], stride)
    placed = jnp.where(chosen[:, None, :, None], values[:, :, None, :], 0.0)
    return placed.reshape(values.shape[0], -1, values.shape[2])


def extract(field, stride):
    chosen = selector(field.shape[0], stride)
    lattice = field.reshape(field.shape[0], -1, stride)
    return jnp.sum(jnp.where(chosen[:, None, :], lattice, 0.0), -1)


def extract_rows(field, stride):
    chosen = selector(field.shape[0], stride)
    lattice = field.reshape(field.shape[0], -1, stride, field.shape[2])
    return jnp.sum(jnp.where(chosen[:, None, :, None], lattice, 0.0), 2)


def local(tiles, tile_pos, lengths, qkv_weight, out_weight, cotangent):
    row_count = tiles.shape[1]
    features = tiles.shape[2]
    peer_count = lax.axis_size("ctx")
    device = lax.axis_index("ctx")
    portion = row_count // peer_count
    number = out_weight.shape[0] // HD
    stride = WIDE_RATE2
    groups = row_count // stride
    places = tile_pos[0]
    ordering = jnp.argsort(places // row_count, stable=True)
    sent_rows = tiles[0][ordering].reshape(peer_count, portion, features)
    sent_places = places[ordering].reshape(peer_count, portion)
    got_rows, got_places = (
        lax.all_to_all(sent_rows, "ctx", split_axis=0, concat_axis=0, tiled=True),
        lax.all_to_all(sent_places, "ctx", split_axis=0, concat_axis=0, tiled=True),
    )
    slot_index = got_places.reshape(row_count) - device * row_count
    sequence = (
        jnp.zeros((row_count, features), jnp.bfloat16)
        .at[slot_index]
        .set(got_rows.reshape(row_count, features))
    )
    projected = jnp.dot(sequence, qkv_weight, preferred_element_type=jnp.float32).astype(
        jnp.bfloat16
    )
    projected = projected.reshape(row_count, 3, number, HD)
    queries = projected[:, 0]
    keyset = projected[:, 1]
    values = projected[:, 2]
    slide_length = lengths[0]
    live_rows = device * row_count + jnp.arange(row_count) < slide_length
    local_scores = (
        jnp.einsum("qhd,khd->hqk", queries, keyset, preferred_element_type=jnp.float32) * 0.125
    )
    local_masked = jnp.where(live_rows[None, None, :], local_scores, NEGATIVE_FLOOR)
    local_max = jnp.max(local_masked, -1)
    near_query = dilate(queries, stride)
    near_keys = dilate(keyset, stride)
    near_values = dilate(values, stride)
    far_keys, far_values = (
        lax.all_gather(near_keys, "ctx", axis=1, tiled=True),
        lax.all_gather(near_values, "ctx", axis=1, tiled=True),
    )
    head_offsets = jnp.arange(number)[:, None]
    far_live = jnp.arange(groups * peer_count)[None, :] * stride + head_offsets < slide_length
    distant_scores = (
        jnp.einsum("hqd,hkd->hqk", near_query, far_keys, preferred_element_type=jnp.float32) * 0.125
    )
    distant_masked = jnp.where(far_live[:, None, :], distant_scores, NEGATIVE_FLOOR)
    far_max = jnp.max(distant_masked, -1)
    ceiling = jnp.maximum(local_max, spread(far_max, stride, NEGATIVE_FLOOR))
    local_weights = jnp.where(
        live_rows[None, None, :], jnp.exp(local_masked - ceiling[:, :, None]), 0.0
    )
    distant_ceiling = extract(ceiling, stride)
    distant_weights = jnp.where(
        far_live[:, None, :], jnp.exp(distant_masked - distant_ceiling[:, :, None]), 0.0
    )
    totals = jnp.sum(local_weights, -1) + spread(jnp.sum(distant_weights, -1), stride, 0.0)
    local_numer = jnp.einsum(
        "hqk,khd->hqd",
        local_weights.astype(jnp.bfloat16),
        values,
        preferred_element_type=jnp.float32,
    )
    far_numer = jnp.einsum(
        "hqk,hkd->hqd",
        distant_weights.astype(jnp.bfloat16),
        far_values,
        preferred_element_type=jnp.float32,
    )
    numerator = local_numer + spread_rows(far_numer, stride)
    divisor = jnp.where(live_rows[None, :], totals, 1.0)
    result = jnp.where(live_rows[None, :, None], numerator / divisor[:, :, None], 0.0)
    attention = result.transpose(1, 0, 2).reshape(row_count, number * HD).astype(jnp.bfloat16)
    grad_seq = cotangent[0]
    factor = 1.0 / math.sqrt(lax.axis_size("slide") * peer_count * row_count)
    partial_term = (
        jnp.einsum("qc,qd->cd", attention, grad_seq, preferred_element_type=jnp.float32) * factor
    )
    weight_grad = lax.psum_scatter(
        partial_term.reshape(-1), ("slide", "ctx"), scatter_dimension=0, tiled=True
    )
    grad_attn = jnp.einsum(
        "qd,cd->qc", grad_seq, out_weight, preferred_element_type=jnp.float32
    ).astype(jnp.bfloat16)
    grad_attn = grad_attn.reshape(row_count, number, HD)
    grad_out = jnp.where(
        live_rows[:, None, None], grad_attn, jnp.zeros((), jnp.bfloat16)
    ).transpose(1, 0, 2)
    inner_stat = jnp.sum(grad_out.astype(jnp.float32) * result, -1)
    local_prob = local_weights / divisor[:, :, None]
    local_dprob = jnp.einsum("hqd,khd->hqk", grad_out, values, preferred_element_type=jnp.float32)
    local_dscore = (local_prob * (local_dprob - inner_stat[:, :, None]) * 0.125).astype(
        jnp.bfloat16
    )
    grad_query = jnp.einsum(
        "hqk,khd->hqd", local_dscore, keyset, preferred_element_type=jnp.float32
    )
    grad_key = jnp.einsum("hqk,qhd->hkd", local_dscore, queries, preferred_element_type=jnp.float32)
    grad_value = jnp.einsum(
        "hqk,hqd->hkd",
        local_prob.astype(jnp.bfloat16),
        grad_out,
        preferred_element_type=jnp.float32,
    )
    near_divisor = extract(divisor, stride)
    near_stat = extract(inner_stat, stride)
    near_grad = extract_rows(grad_out.astype(jnp.float32), stride).astype(jnp.bfloat16)
    far_prob = distant_weights / near_divisor[:, :, None]
    far_dprob = jnp.einsum(
        "hqd,hkd->hqk", near_grad, far_values, preferred_element_type=jnp.float32
    )
    far_dscore = (far_prob * (far_dprob - near_stat[:, :, None]) * 0.125).astype(jnp.bfloat16)
    far_qgrad = jnp.einsum("hqk,hkd->hqd", far_dscore, far_keys, preferred_element_type=jnp.float32)
    grad_query = grad_query + spread_rows(far_qgrad, stride)
    partial_keys = jnp.einsum(
        "hqk,hqd->hkd", far_dscore, near_query, preferred_element_type=jnp.float32
    )
    partial_values = jnp.einsum(
        "hqk,hqd->hkd", far_prob.astype(jnp.bfloat16), near_grad, preferred_element_type=jnp.float32
    )
    owned_kgrad, owned_vgrad = (
        lax.psum_scatter(partial_keys, "ctx", scatter_dimension=1, tiled=True),
        lax.psum_scatter(partial_values, "ctx", scatter_dimension=1, tiled=True),
    )
    grad_key = grad_key + spread_rows(owned_kgrad, stride)
    grad_value = grad_value + spread_rows(owned_vgrad, stride)
    far_pair = jnp.stack([owned_kgrad, owned_vgrad], 0) * math.sqrt(groups * peer_count)
    stacked = jnp.stack([grad_query, grad_key, grad_value], 0).transpose(2, 0, 1, 3)
    stacked = stacked.reshape(row_count, 3 * number * HD).astype(jnp.bfloat16)
    grad_rows = jnp.einsum(
        "qc,dc->qd", stacked, qkv_weight, preferred_element_type=jnp.float32
    ).astype(jnp.bfloat16)
    back_rows = grad_rows[slot_index].reshape(peer_count, portion, features)
    returned = lax.all_to_all(back_rows, "ctx", split_axis=0, concat_axis=0, tiled=True)
    tile_grads = (
        jnp.zeros((row_count, features), jnp.bfloat16)
        .at[ordering]
        .set(returned.reshape(row_count, features))
    )
    return (tile_grads[None], weight_grad, far_pair[None])


def solution(mesh):
    placed = (
        P("slide", "ctx", None),
        P("slide", "ctx"),
        P("slide"),
        P(),
        P(),
        P("slide", "ctx", None),
    )
    return jax.shard_map(
        local,
        mesh=mesh,
        in_specs=placed,
        out_specs=(
            P("slide", "ctx", None),
            P(("slide", "ctx")),
            P("slide", None, None, "ctx", None),
        ),
        check_vma=False,
    )
```

profile of v0, /device:TPU:1, one launch (start us, length us, event | category | flops | bytes accessed | tf_op | source)
XLA Modules:
  0.0 875.4 jit_solution(16452067823011746437)
XLA Ops:
  8.9 3.8 sort.17
  13.2 3.6 gather_fusion
  17.5 10.4 %all-to-all-start = ((s32[32,1,16]{2,1,0:T(1,128)}), s32[32,1,16]{2,1,0:T(1,128)S(1)}, u32[]{:S(2)}, u32[]{:S(2)}) async-start(s32[32,1,16]{2,1,0:T(1,128)} %bitcast.2), calls=%async_computation | async-start | bytes 32768 | tf_op jit(solution)/shard_map/all_to_all | solution.py:63
  28.6 1.8 convolution_convert_fusion.2
  32.7 2.7 gather_fusion.1
  35.4 7.5 all-to-all-start.1
  46.0 11.3 %all-to-all-done.1 = bf16[32,16,768]{2,1,0:T(8,128)(2,1)} async-done(((bf16[32,16,768]{2,1,0:T(8,128)(2,1)}), bf16[32,16,768]{2,1,0:T(8,128)(2,1)}, u32[]{:S(2)}, u32[]{:S(2)}) %all-to-all-start.1) | async-done | bytes 786464 | tf_op jit(solution)/shard_map/all_to_all | solution.py:62
  57.2 3.4 scatter_custom_fusion
  60.7 2.2 convolution_convert_fusion
  65.6 4.1 fusion
  73.9 23.6 %all_gather.6 = bf16[6,1024,64]{2,1,0:T(8,128)(2,1)S(1)} all-gather(bf16[6,32,64]{2,1,0:T(8,128)(2,1)S(1)} %constant_dynamic-update-slice_fusion.6), channel_id=1, replica_groups=mesh['slide'=16,'ctx'=32] {'ctx'}, dimensions={1}, use_global_device_ids=true | all-gather | bytes 811008 | tf_op jit(solution)/shard_map/all_gather | solution.py:89
  102.6 27.0 %all_gather.7 = bf16[6,1024,64]{2,1,0:T(8,128)(2,1)} all-gather(bf16[6,32,64]{2,1,0:T(8,128)(2,1)S(1)} %constant_dynamic-update-slice_fusion.12), channel_id=1, replica_groups=mesh['slide'=16,'ctx'=32] {'ctx'}, dimensions={1}, use_global_device_ids=true | all-gather | bytes 811008 | tf_op jit(solution)/shard_map/all_gather | solution.py:90
  133.5 4.5 fusion.73
  138.1 2.1 fusion.36
  141.4 2.8 copy.95
  144.2 6.2 fusion.75
  153.3 3.7 fusion.47
  157.7 2.2 fusion.20
  162.2 3.4 fusion.81
  165.7 5.0 multiply_convert_fusion
  173.0 85.1 %reduce-scatter.5.cloned.1.call-done = f32[6,32,64]{2,1,0:T(8,128)} async-done(((f32[6,1024,64]{2,1,0:T(8,128)}), f32[6,32,64]{2,1,0:T(8,128)}) %reduce-scatter.5.cloned.1.call-update) | async-done | bytes 49168 | tf_op jit(solution)/shard_map/reduce_scatter | solution.py:173
  258.2 2.1 broadcast_in_dim.331
  260.3 2.7 copy.103
  263.0 5.9 fusion.28
  269.0 97.3 %reduce-scatter.3.cloned.1.call-done = f32[6,32,64]{2,1,0:T(8,128)} async-done(((f32[6,1024,64]{2,1,0:T(8,128)}), f32[6,32,64]{2,1,0:T(8,128)}) %reduce-scatter.3.cloned.1.call-update) | async-done | bytes 49168 | tf_op jit(solution)/shard_map/reduce_scatter | solution.py:172
  366.3 2.2 broadcast_in_dim.329
  368.4 2.7 copy.101
  371.2 3.2 fusion.27
  375.8 2.7 gather_fusion.2
  378.5 7.3 all-to-all-start.2
  389.0 472.8 %all-reduce.3.cloned.1.call-done = f32[294912]{0:T(1024)} async-done(((f32[294912]{0:T(1024)}), f32[294912]{0:T(1024)}) %all-reduce.3.cloned.1.call-update) | async-done | bytes 1179664
  863.9 4.1 scatter_custom_fusion.1
  (143 shorter events, 38.9 us)
Async XLA Ops:
  8.0 52.7 %copy-start = (bf16[768,1152]{1,0:T(8,128)(2,1)S(1)}, bf16[768,1152]{1,0:T(8,128)(2,1)}, u32[]{:S(2)}) copy-start(bf16[768,1152]{1,0:T(8,128)(2,1)} %param.9) | copy-start | bytes 5308420
  8.0 24.7 %copy-start.1 = (bf16[1,512,768]{2,1,0:T(8,128)(2,1)S(1)}, bf16[1,512,768]{2,1,0:T(8,128)(2,1)}, u32[]{:S(2)}) copy-start(bf16[1,512,768]{2,1,0:T(8,128)(2,1)} %param.6) | copy-start | bytes 2359300
  17.5 17.9 %all-to-all-start = ((s32[32,1,16]{2,1,0:T(1,128)}), s32[32,1,16]{2,1,0:T(1,128)S(1)}, u32[]{:S(2)}, u32[]{:S(2)}) async-start(s32[32,1,16]{2,1,0:T(1,128)} %bitcast.2), calls=%async_computation | async-start | bytes 32768 | tf_op jit(solution)/shard_map/all_to_all | solution.py:63
  28.6 37.0 %copy-start.26 = (pred[512]{0:T(512)(128)(4,1)}, pred[512]{0:T(512)(128)(4,1)S(1)}, u32[]{:S(2)}) copy-start(pred[512]{0:T(512)(128)(4,1)S(1)} %add_compare_fusion.2) | copy-start | bytes 1540
  35.4 21.8 %all-to-all-start.1 = ((bf16[32,16,768]{2,1,0:T(8,128)(2,1)}), bf16[32,16,768]{2,1,0:T(8,128)(2,1)}, u32[]{:S(2)}, u32[]{:S(2)}) async-start(bf16[32,16,768]{2,1,0:T(8,128)(2,1)} %bitcast.5), calls=%async_computation.1 | async-start | bytes 1572864 | tf_op jit(solution)/shard_map/all_to_all | solution.py:62
  43.0 215.2 %reduce-scatter.5.cloned.1.call-start = ((), (), s32[]{:S(2)}) async-start(), calls=%async_computation.6 | async-start | bytes 3244032 | tf_op jit(solution)/shard_map/reduce_scatter | solution.py:173
  43.0 2.8 copy-start.23
  46.0 16.9 %copy-start.30 = (s32[512,1]{0,1:T(1,128)}, s32[512,1]{0,1:T(1,128)S(1)}, u32[]{:S(2)}) copy-start(s32[512,1]{0,1:T(1,128)S(1)} %compare_select_fusion) | copy-start | bytes 6148
  64.5 5.2 copy-start.2
  97.5 1.5 copy-start.13
  133.5 10.8 %copy-start.16 = (f32[6,512]{1,0:T(8,128)}, f32[6,512]{1,0:T(8,128)S(1)}, u32[]{:S(2)}) copy-start(f32[6,512]{1,0:T(8,128)S(1)} %select_maximum_fusion) | copy-start | bytes 36868
  133.5 4.6 copy-start.27
  138.1 6.2 copy-start.21
  153.3 4.0 copy-start.31
  153.3 4.0 copy-start.15
  153.3 4.0 copy-start.32
  157.1 209.2 %reduce-scatter.3.cloned.1.call-start = ((), (), s32[]{:S(2)}) async-start(), calls=%async_computation.5 | async-start | bytes 3244032 | tf_op jit(solution)/shard_map/reduce_scatter | solution.py:172
  160.0 2.2 copy-start.14
  162.2 3.5 copy-start.3
  162.2 3.5 copy-start.12
  162.2 3.5 copy-start.17
  162.2 3.5 copy-start.20
  162.2 3.5 copy-start.22
  162.2 3.5 copy-start.28
  165.7 6.7 copy-start.5
  170.8 1.6 copy-start.4
  371.2 3.2 copy-start.8
  375.8 10.4 %copy-start.7 = (bf16[6,512,64]{1,2,0:T(8,128)(2,1)S(1)}, bf16[6,512,64]{1,2,0:T(8,128)(2,1)}, u32[]{:S(2)}) copy-start(bf16[6,512,64]{1,2,0:T(8,128)(2,1)} %get-tuple-element.10) | copy-start | bytes 1179652
  378.5 485.4 %all-to-all-start.2 = ((bf16[32,16,768]{2,1,0:T(8,128)(2,1)}), bf16[32,16,768]{2,1,0:T(8,128)(2,1)}, u32[]{:S(2)}, u32[]{:S(2)}) async-start(bf16[32,16,768]{2,1,0:T(8,128)(2,1)} %bitcast.45), calls=%async_computation.4 | async-start | bytes 1572864 | tf_op jit(solution)/shard_map/all_to_all | solution.py:184
  385.9 477.3 %copy-start.9 = (f32[6,32,64]{2,1,0:T(8,128)S(1)}, f32[6,32,64]{2,1,0:T(8,128)}, u32[]{:S(2)}) copy-start(f32[6,32,64]{2,1,0:T(8,128)} %reduce-scatter.5.cloned.1.call-done) | copy-start | bytes 147460
  385.9 477.3 %copy-start.10 = (f32[6,32,64]{2,1,0:T(8,128)S(1)}, f32[6,32,64]{2,1,0:T(8,128)}, u32[]{:S(2)}) copy-start(f32[6,32,64]{2,1,0:T(8,128)} %reduce-scatter.3.cloned.1.call-done) | copy-start | bytes 147460
  385.9 475.9 %all-reduce.3.cloned.1.call-start = ((), (), s32[]{:S(2)}) async-start(), calls=%async_computation.7 | async-start | bytes 2359296
  (7 other events, 4.5 us)
Sparse Core Ops, SparseCore 0:
  157.2 100.9 reduce-scatter.4
  263.3 102.9 reduce-scatter.2
Sparse Core Ops, SparseCore 1:
  391.8 470.0 all-reduce.2
where the time goes:
time: 878 us; the launch traced here: 875 us
  waiting for transfers between devices  667 us (76%)
  local copies, waits for them, and re-layouts  53.2 us (6%)
  blocking collectives  50.6 us (6%)
  matrix products  45.3 us (5%)
  starting transfers between devices  25.9 us (3%)
  other arithmetic  17.1 us (2%)
  between operations  16.8 us (2%)
    unnamed x4, waiting for transfers between devices  473 us
    reduce_scatter x1, waiting for transfers between devices, local(): lax.psum_scatter(partial_keys, 'ctx', scatter_dimension=1, tiled=True)  97.3 us
    reduce_scatter x1, waiting for transfers between devices, local(): lax.psum_scatter(partial_values, 'ctx', scatter_dimension=1, tiled=True)  85.1 us
    all_gather x1, blocking collectives, local(): lax.all_gather(near_values, 'ctx', axis=1, tiled=True)  27 us
    all_gather x1, blocking collectives, local(): lax.all_gather(near_keys, 'ctx', axis=1, tiled=True)  23.6 us
  transfers between devices with their start and end apart: 6, of which 4 were waited for; matrix products, arithmetic and copies ran while one was open for 4% of the time, Pallas kernels for 0%

commit v1 on v0

v1 whole, which is shorter than its diff:
```python
import math

import jax
import jax.numpy as jnp
from jax import lax
from jax.experimental import pallas as pl
from jax.experimental.pallas import tpu as pltpu
from jax.sharding import PartitionSpec as P

HD = 64
HEADS = 6
STRIDE = 16
PEERS = 32
ROWS = 512
PORTION = 16
GROUPS = ROWS // STRIDE
FAR = HEADS * GROUPS
WIDTH = 768
INNER = HEADS * HD
QUERIES = 8 * GROUPS
KEYS = PEERS * GROUPS
CHUNK = GROUPS + 8
PIECE = 640
FLOOR = -1e30
SCALE = 0.125
LOG_SCALE = 0.125 * math.log2(math.e)
BF = jnp.bfloat16
F32 = jnp.float32


def nn(a, b):
    return lax.dot_general(a, b, (((1,), (0,)), ((), ())), preferred_element_type=F32)


def nt(a, b):
    return lax.dot_general(a, b, (((1,), (1,)), ((), ())), preferred_element_type=F32)


def tn(a, b):
    return lax.dot_general(a, b, (((0,), (0,)), ((), ())), preferred_element_type=F32)


def iota(shape, dim):
    return lax.broadcasted_iota(jnp.int32, shape, dim)


def mark(mask):
    return jnp.where(mask, 1.0, 0.0).astype(BF)


def split3(x):
    high = x.astype(BF)
    rest = x - high.astype(F32)
    middle = rest.astype(BF)
    low = (rest - middle.astype(F32)).astype(BF)
    return high.astype(F32), middle.astype(F32), low.astype(F32)


def key_bias(count, live):
    return jnp.where(iota((1, count), 1) < live, 0.0, FLOOR)


def far_rows():
    r = iota((FAR, ROWS), 0)
    return mark(((r & (GROUPS - 1)) * STRIDE + (r >> 5)) == iota((FAR, ROWS), 1))


def own_head():
    return (iota((FAR, INNER), 0) >> 5) == (iota((FAR, INNER), 1) >> 6)


def fold(offset):
    return mark((iota((INNER, 128), 0) & (HD - 1)) + offset == iota((INNER, 128), 1))


def pack_kernel(pos_ref, tiles_ref, send_ref, slot_ref):
    places = pos_ref[...]
    block = places >> 9
    member = iota((PEERS, ROWS), 0) == block
    before = mark(iota((ROWS, ROWS), 0) < iota((ROWS, ROWS), 1))
    counts = nn(mark(member), before)
    rank = jnp.sum(jnp.where(member, counts, 0.0), 0, keepdims=True)
    slot = block * PORTION + rank.astype(jnp.int32)
    slot_ref[...] = slot
    order = mark(iota((ROWS, ROWS), 0) == slot)
    send_ref[:, :WIDTH] = nn(order, tiles_ref[...]).astype(BF)
    inside = places & (ROWS - 1)
    line = iota((128, ROWS), 0)
    code = jnp.where(line == 0, inside >> 4, jnp.where(line == 1, inside & 15, 0))
    send_ref[:, WIDTH:] = nt(order, code.astype(F32).astype(BF)).astype(BF)


def project_kernel(
    scal_ref, recv_ref, weight_ref, grad_ref, proj_ref, far_ref, fgrad_ref, mean_ref, lse_ref, send_ref
):
    lane = iota((8, 128), 1)
    pick = jnp.where(iota((8, 128), 0) == 0, jnp.where(lane == 0, 16.0, jnp.where(lane == 1, 1.0, 0.0)), 0.0)
    place = nt(pick.astype(BF), recv_ref[:, WIDTH:])[0:1].astype(jnp.int32)
    order = mark(iota((ROWS, ROWS), 0) == place)
    sequence = nn(order, recv_ref[:, :WIDTH]).astype(BF)
    proj = nn(sequence, weight_ref[...]).astype(BF)
    proj_ref[...] = proj
    chosen = far_rows()
    own = own_head()
    far = nn(chosen, proj)
    fq = jnp.where(own, far[:, :INNER], 0.0).astype(BF)
    fk = jnp.where(own, far[:, INNER : 2 * INNER], 0.0).astype(BF)
    fv = jnp.where(own, far[:, 2 * INNER :], 0.0).astype(BF)
    fgrad = jnp.where(own, nn(chosen, grad_ref[...]), 0.0).astype(BF)
    far_ref[...] = fq
    fgrad_ref[...] = fgrad
    scores = nt(fq, proj[:, INNER : 2 * INNER]) * LOG_SCALE + key_bias(ROWS, scal_ref[0])
    top = jnp.max(scores, -1, keepdims=True)
    weight = jnp.exp2(scores - top)
    total = jnp.sum(weight, -1, keepdims=True)
    mean = jnp.where(own, nn(weight.astype(BF), proj[:, 2 * INNER :]) / total, 0.0)
    mean_ref[...] = mean
    lse = top + jnp.log2(total)
    lse_ref[...] = jnp.broadcast_to(lse, (FAR, 128))
    inner = jnp.sum(fgrad.astype(F32) * mean, -1, keepdims=True)
    first, second = fold(0), fold(HD)
    key_value = (nn(fk, first) + nn(fv, second)).astype(BF)
    query_grad = (nn(fq, first) + nn(fgrad, second)).astype(BF)
    column = iota((FAR, 128), 1)
    stats = jnp.zeros((FAR, 128), F32)
    for at, part in enumerate(split3(lse) + split3(inner)):
        stats = jnp.where(column == at, part, stats)
    stats = jnp.concatenate([stats, jnp.zeros((QUERIES - FAR, 128), F32)], 0).astype(BF)
    stats = nt(mark(iota((8, 128), 0) == iota((8, 128), 1)), stats).astype(BF)
    for peer in range(PEERS):
        head = (peer % 8) % HEADS
        rows = slice(head * GROUPS, (head + 1) * GROUPS)
        send_ref[peer, :GROUPS, :128] = key_value[rows]
        send_ref[peer, :GROUPS, 128:] = query_grad[rows]
        send_ref[peer, GROUPS:, :] = stats


def local_kernel(scal_ref, q_ref, k_ref, v_ref, grad_ref, att_ref, dq_ref, dk_ref, dv_ref):
    pair = pl.program_id(0)
    live = scal_ref[0]
    bias = key_bias(ROWS, live)
    q, k, v, grad = q_ref[...], k_ref[...], v_ref[...], grad_ref[...]
    row = iota((ROWS, 128), 0)
    side = iota((ROWS, 128), 1) >> 6
    zero = jnp.zeros((), BF)
    atts, dqs, dks, dvs = [], [], [], []
    for half in range(2):
        ours = side == half
        kept = ours & ((row & (STRIDE - 1)) != pair * 2 + half)
        query = jnp.where(ours, q, zero)
        out_grad = jnp.where(kept, grad, zero)
        scores = nt(query, k) * LOG_SCALE + bias
        weight = jnp.exp2(scores - jnp.max(scores, -1, keepdims=True))
        inverse = 1.0 / jnp.sum(weight, -1, keepdims=True)
        result = jnp.where(kept & (row < live), nn(weight.astype(BF), v) * inverse, 0.0)
        stat = jnp.sum(out_grad.astype(F32) * result, -1, keepdims=True)
        prob = weight * inverse
        dscore = (prob * (nt(out_grad, v) - stat) * SCALE).astype(BF)
        atts.append(result)
        dqs.append(jnp.where(kept, nn(dscore, k), 0.0))
        dks.append(tn(dscore, query))
        dvs.append(tn(prob.astype(BF), out_grad))
    att_ref[...] = (atts[0] + atts[1]).astype(BF)
    dq_ref[...] = (dqs[0] + dqs[1]).astype(BF)
    dk_ref[...] = dks[0] + dks[1]
    dv_ref[...] = dvs[0] + dvs[1]


def far_kernel(scal_ref, recv_ref, send_ref):
    first = scal_ref[2] * 8
    head = scal_ref[3]
    kv = recv_ref[:, :GROUPS, :128].reshape(KEYS, 128)
    mine = recv_ref[pl.ds(first, 8), :GROUPS, 128:].reshape(QUERIES, 128)
    pick = mark(iota((GROUPS, QUERIES), 1) == iota((GROUPS, QUERIES), 0) + head * GROUPS)
    parts = [nt(pick, recv_ref[first + j, GROUPS:, :]) for j in range(8)]
    parts = jnp.concatenate(parts, 0)
    lse = parts[:, 0:1] + parts[:, 1:2] + parts[:, 2:3]
    inner = parts[:, 3:4] + parts[:, 4:5] + parts[:, 5:6]
    left = iota((QUERIES, 128), 1) < HD
    zero = jnp.zeros((), BF)
    query = jnp.where(left, mine, zero)
    grad = jnp.where(left, zero, mine)
    alive = iota((1, KEYS), 1) * STRIDE + head < scal_ref[1]
    scores = nt(query, kv) * LOG_SCALE + jnp.where(alive, 0.0, FLOOR)
    top = jnp.max(scores, -1, keepdims=True)
    weight = jnp.exp2(scores - top)
    ceiling = jnp.maximum(top, lse)
    gain = jnp.exp2(top - ceiling)
    near = jnp.exp2(lse - ceiling)
    inverse = 1.0 / (jnp.sum(weight, -1, keepdims=True) * gain + near)
    gain = gain * inverse
    share = near * inverse
    numerator = nn(weight.astype(BF), kv) * gain
    stat = jnp.sum(grad.astype(F32) * numerator, -1, keepdims=True) + share * inner
    prob = weight * gain
    dscore = (prob * (nt(grad, kv) - stat) * SCALE).astype(BF)
    query_out = jnp.where(left, nn(dscore, kv), numerator).astype(BF)
    key_left = iota((KEYS, 128), 1) < HD
    key_out = jnp.where(key_left, tn(dscore, mine), tn(prob.astype(BF), mine)).astype(BF)
    column = iota((QUERIES, 128), 1)
    stats = jnp.zeros((QUERIES, 128), F32)
    for at, part in enumerate(split3(share)):
        stats = jnp.where(column == at, part, stats)
    stats = nt(mark(iota((8, 128), 0) == iota((8, 128), 1)), stats.astype(BF)).astype(BF)
    for peer in range(PEERS):
        j = peer % 8
        send_ref[peer, :GROUPS, :128] = key_out[peer * GROUPS : (peer + 1) * GROUPS]
        send_ref[peer, :GROUPS, 128:] = query_out[j * GROUPS : (j + 1) * GROUPS]
        send_ref[peer, GROUPS:, :] = stats


def returned_far(scal_ref, recv_ref):
    first = scal_ref[2] * 8
    pick = mark(iota((GROUPS, QUERIES), 1) == iota((GROUPS, QUERIES), 0) + scal_ref[4] * GROUPS)
    shares = jnp.concatenate([nt(pick, recv_ref[first + h, GROUPS:, :]) for h in range(HEADS)], 0)
    share = shares[:, 0:1] + shares[:, 1:2] + shares[:, 2:3]
    query_out = jnp.concatenate([recv_ref[first + h, :GROUPS, 128:] for h in range(HEADS)], 0)
    return share, query_out


def far_result(scal_ref, share, query_out, mean):
    r = iota((FAR, INNER), 0)
    live = (r & (GROUPS - 1)) * STRIDE + (r >> 5) < scal_ref[0]
    numerator = nt(query_out, fold(HD))
    return jnp.where(live & own_head(), numerator + share * mean, 0.0)


def weight_kernel(scal_ref, recv_ref, mean_ref, att_ref, cot_ref, send_ref):
    share, query_out = returned_far(scal_ref, recv_ref)
    result = far_result(scal_ref, share, query_out, mean_ref[...]).astype(BF)
    attention = att_ref[...] + tn(far_rows(), result).astype(BF)
    new = iota((INNER, INNER), 1)
    old = 3 * (8 * (new & 15) + ((new >> 4) & 7)) + (new >> 7)
    attention = nn(attention, mark(iota((INNER, INNER), 0) == old)).astype(BF)
    terms = (tn(attention, cot_ref[...]) * (1.0 / 512.0)).astype(BF)
    one, two, three = terms[:128], terms[128:256], terms[256:]
    pieces = (
        one[:, :PIECE],
        jnp.concatenate([one[:, 512:], two[:, :384]], 1),
        jnp.concatenate([two[:, 384:], three[:, :256]], 1),
        three[:, 128:],
    )
    for r in range(4):
        for q in range(8):
            send_ref[4 * q + r] = pieces[r][16 * q : 16 * q + 16]


def finish_kernel(
    scal_ref,
    recv_ref,
    proj_ref,
    far_ref,
    fgrad_ref,
    mean_ref,
    lse_ref,
    dq_ref,
    dk_ref,
    dv_ref,
    weight_ref,
    code_ref,
    back_ref,
    pair_ref,
):
    share, query_out = returned_far(scal_ref, recv_ref)
    result = far_result(scal_ref, share, query_out, mean_ref[...])
    fq, fgrad = far_ref[...], fgrad_ref[...]
    keys, values = proj_ref[:, INNER : 2 * INNER], proj_ref[:, 2 * INNER :]
    stat = jnp.sum(fgrad.astype(F32) * result, -1, keepdims=True)
    scores = nt(fq, keys) * LOG_SCALE + key_bias(ROWS, scal_ref[0])
    prob = jnp.exp2(scores - lse_ref[:, 0:1]) * share
    dscore = (prob * (nt(fgrad, values) - stat) * SCALE).astype(BF)
    own = own_head()
    chosen = far_rows()
    far_dq = jnp.where(own, nn(dscore, keys) + nt(query_out, fold(0)), 0.0).astype(BF)
    pairs = []
    for h in range(HEADS):
        total = recv_ref[h, :GROUPS, :128].astype(F32)
        for b in range(1, 4):
            total = total + recv_ref[8 * b + h, :GROUPS, :128].astype(F32)
        pairs.append(total)
    pairs = jnp.concatenate(pairs, 0)
    scaled = pairs * 32.0
    pair_ref[0] = scaled[:, :HD]
    pair_ref[1] = scaled[:, HD:]
    high = pairs.astype(BF)
    low = (pairs - high.astype(F32)).astype(BF)
    zero = jnp.zeros((), F32)

    def placed(offset):
        table = fold(offset)
        upper = jnp.where(own, nt(high, table), zero).astype(BF)
        lower = jnp.where(own, nt(low, table), zero).astype(BF)
        return tn(chosen, upper) + tn(chosen, lower)

    grad_query = dq_ref[...] + tn(chosen, far_dq).astype(BF)
    grad_key = (dk_ref[...] + tn(dscore, fq) + placed(0)).astype(BF)
    grad_value = (dv_ref[...] + tn(prob.astype(BF), fgrad) + placed(HD)).astype(BF)
    rows = nt(grad_query, weight_ref[:, :INNER])
    rows = rows + nt(grad_key, weight_ref[:, INNER : 2 * INNER])
    rows = rows + nt(grad_value, weight_ref[:, 2 * INNER :])
    code = code_ref[...].astype(F32)
    place = (code[:, 0:1] * 16.0 + code[:, 1:2]).astype(jnp.int32)
    order = mark(iota((ROWS, ROWS), 1) == place)
    back_ref[...] = nn(order, rows.astype(BF)).astype(BF)


def unpack_kernel(slot_ref, rows_ref, out_ref):
    order = mark(iota((ROWS, ROWS), 0) == slot_ref[...])
    out_ref[...] = tn(order, rows_ref[...]).astype(BF)


def call(body, outs, flops, name, **rest):
    return pl.pallas_call(
        body,
        out_shape=outs,
        name=name,
        compiler_params=pltpu.CompilerParams(vmem_limit_bytes=40 * 1024 * 1024),
        cost_estimate=pl.CostEstimate(flops=flops, bytes_accessed=4_000_000, transcendentals=0),
        **rest,
    )


def shape(dims, dtype=BF):
    return jax.ShapeDtypeStruct(dims, dtype)


def exchange(rows, axis):
    return lax.all_to_all(rows, axis, split_axis=0, concat_axis=0, tiled=True)


SMEM = pl.BlockSpec(memory_space=pltpu.SMEM)
WHOLE = pl.BlockSpec(memory_space=pltpu.VMEM)


def local(tiles, tile_pos, lengths, qkv_weight, out_weight, cotangent):
    device = lax.axis_index("ctx")
    length = lengths[0]
    live = length - device * ROWS
    scal = jnp.stack([live, length, device // 8, (device % 8) % HEADS, device % 8]).astype(jnp.int32)
    cot = cotangent[0]

    sent, slot = call(pack_kernel, (shape((ROWS, 896)), shape((1, ROWS), jnp.int32)), 800_000_000, "pack")(
        tile_pos, tiles[0]
    )
    got = exchange(sent.reshape(PEERS, PORTION, 896), "ctx").reshape(ROWS, 896)

    grad_attn = jnp.einsum("qd,cd->qc", cot, out_weight, preferred_element_type=F32).astype(BF)
    alive = lax.broadcasted_iota(jnp.int32, (ROWS, 1), 0) < live
    grad_out = jnp.where(alive, grad_attn, jnp.zeros((), BF))

    proj, far_q, far_grad, mean, lse, far_sent = call(
        project_kernel,
        (
            shape((ROWS, 3 * INNER)),
            shape((FAR, INNER)),
            shape((FAR, INNER)),
            shape((FAR, INNER), F32),
            shape((FAR, 128), F32),
            shape((PEERS, CHUNK, 256)),
        ),
        3_000_000_000,
        "project",
        in_specs=[SMEM, WHOLE, WHOLE, WHOLE],
    )(scal, got, qkv_weight, grad_out)
    far_got = exchange(far_sent, "ctx")

    def columns(base):
        return pl.BlockSpec((ROWS, 128), lambda t: (0, base + t))

    att, dq, dk, dv = call(
        local_kernel,
        (shape((ROWS, INNER)), shape((ROWS, INNER)), shape((ROWS, INNER), F32), shape((ROWS, INNER), F32)),
        12_000_000_000,
        "local_rows",
        grid=(3,),
        in_specs=[SMEM, columns(0), columns(3), columns(6), columns(0)],
        out_specs=(columns(0),) * 4,
    )(scal, proj, proj, proj, grad_out)

    far_back = call(far_kernel, shape((PEERS, CHUNK, 256)), 3_000_000_000, "far", in_specs=[SMEM, WHOLE])(
        scal, far_got
    )
    far_back = exchange(far_back, "ctx")

    pieces = call(
        weight_kernel,
        shape((PEERS, 16, PIECE)),
        1_000_000_000,
        "weight",
        in_specs=[SMEM, WHOLE, WHOLE, WHOLE, WHOLE],
    )(scal, far_back, mean, att, cot)
    pieces = exchange(pieces, "ctx")
    pieces = jnp.sum(pieces.astype(F32), 0)
    pieces = exchange(pieces, "slide")
    pieces = jnp.sum(pieces, 0)
    weight_grad = lax.dynamic_slice(pieces, (HD * (device % 2),), (576,))

    back, pair = call(
        finish_kernel,
        (shape((ROWS, WIDTH)), shape((2, FAR, HD), F32)),
        4_000_000_000,
        "finish",
        grid=(1,),
        in_specs=[SMEM]
        + [pl.BlockSpec(s, lambda t, n=len(s): (0,) * n) for s in ((PEERS, CHUNK, 256), (ROWS, 3 * INNER))]
        + [pl.BlockSpec((FAR, INNER), lambda t: (0, 0))] * 3
        + [pl.BlockSpec((FAR, 128), lambda t: (0, 0))]
        + [pl.BlockSpec((ROWS, INNER), lambda t: (0, 0))] * 3
        + [pl.BlockSpec((WIDTH, 3 * INNER), lambda t: (0, 0)), pl.BlockSpec((ROWS, 128), lambda t: (0, 6))],
        out_specs=(
            pl.BlockSpec((ROWS, WIDTH), lambda t: (0, 0)),
            pl.BlockSpec((2, FAR, HD), lambda t: (0, 0, 0)),
        ),
    )(scal, far_back, proj, far_q, far_grad, mean, lse, dq, dk, dv, qkv_weight, got)
    returned = exchange(back.reshape(PEERS, PORTION, WIDTH), "ctx").reshape(ROWS, WIDTH)
    tile_grads = call(unpack_kernel, shape((ROWS, WIDTH)), 400_000_000, "unpack")(slot, returned)
    return (tile_grads[None], weight_grad, pair.reshape(1, 2, HEADS, GROUPS, HD))


def solution(mesh):
    placed = (
        P("slide", "ctx", None),
        P("slide", "ctx"),
        P("slide"),
        P(),
        P(),
        P("slide", "ctx", None),
    )
    return jax.shard_map(
        local,
        mesh=mesh,
        in_specs=placed,
        out_specs=(
            P("slide", "ctx", None),
            P(("slide", "ctx")),
            P("slide", None, None, "ctx", None),
        ),
        check_vma=False,
    )
```

time: 878 us -> 146 us (0.17)
  waiting for transfers between devices: 667 us -> 38 us
  matrix products: 45.3 us -> 0.6 us
  local copies, waits for them, and re-layouts: 53.2 us -> 18.1 us
  blocking collectives: 50.6 us -> 16.4 us
  Pallas kernels: 0 us -> 27.4 us
  other arithmetic: 17.1 us -> 1.24 us
  starting transfers between devices: 25.9 us -> 41.6 us
  between operations: 16.8 us -> 1.5 us
    unnamed x4 -> x0, waiting for transfers between devices: 473 us -> none
    reduce_scatter x2 -> x0, waiting for transfers between devices: 182 us -> none  [the longest x1 97.3 us: local(): lax.psum_scatter(partial_keys, 'ctx', scatter_dimension=1, tiled=True)]
    all_gather x2 -> x0, blocking collectives: 50.6 us -> none  [the longest x1 27 us: local(): lax.all_gather(near_values, 'ctx', axis=1, tiled=True)]
    dot_general x16 -> x1, matrix products: 45.3 us -> 0.6 us  [local(): jnp.einsum('qd,cd->qc', cot, out_weight, preferred_element_type=F32)]
    pallas_call x0 -> x7, Pallas kernels: none -> 27.4 us  [the longest x1 8.68 us: local(): call(local_kernel, (shape((ROWS, INNER)), shape((ROWS, INNER)), shape((RO...]
    all_to_all x3 -> x5, waiting for transfers between devices: 11.3 us -> 38 us  [exchange(): return lax.all_to_all(rows, axis, split_axis=0, concat_axis=0, tiled=True)]
    all_to_all x3 -> x5, starting transfers between devices: 25.2 us -> 41.6 us  [exchange(): return lax.all_to_all(rows, axis, split_axis=0, concat_axis=0, tiled=True)]
    broadcast_in_dim x14 -> x0, local copies, waits for them, and re-layouts: 16.4 us -> none  [the longest x8 15.3 us: spread_rows(): placed = jnp.where(chosen[:, None, :, None], values[:, :, None, :], 0.0)]
  transfers between devices with their start and end apart: 6 -> 5, of which waited for: 4 -> 4; matrix products, arithmetic and copies ran while one was open for 4% -> 1% of each run, Pallas kernels for 0% -> 11%
where the time goes in v1:
time: 146 us; the launch traced here: 145 us
  starting transfers between devices  41.6 us (28%)
  waiting for transfers between devices  38 us (26%)
  Pallas kernels  27.4 us (19%)
  local copies, waits for them, and re-layouts  18.1 us (12%)
  blocking collectives  16.4 us (11%)
  between operations  1.5 us (1%)
    all_to_all x5, starting transfers between devices, exchange(): return lax.all_to_all(rows, axis, split_axis=0, concat_axis=0, tiled=True)  41.6 us
    all_to_all x5, waiting for transfers between devices, exchange(): return lax.all_to_all(rows, axis, split_axis=0, concat_axis=0, tiled=True)  38 us
    unnamed x48, local copies, waits for them, and re-layouts  16.7 us
    all_to_all x1, blocking collectives, exchange(): return lax.all_to_all(rows, axis, split_axis=0, concat_axis=0, tiled=True)  16.4 us
    pallas_call x1, Pallas kernels, local(): call(local_kernel, (shape((ROWS, INNER)), shape((ROWS, INNER)), shape((RO...  8.68 us
    pallas_call x1, Pallas kernels, local(): call(finish_kernel, (shape((ROWS, WIDTH)), shape((2, FAR, HD), F32)), 400...  6 us
    pallas_call x1, Pallas kernels, local(): call(project_kernel, (shape((ROWS, 3 * INNER)), shape((FAR, INNER)), shap...  3.32 us
    pallas_call x1, Pallas kernels, local(): call(far_kernel, shape((PEERS, CHUNK, 256)), 3000000000, 'far', in_specs=...  3.18 us
  transfers between devices with their start and end apart: 5, of which 4 were waited for; matrix products, arithmetic and copies ran while one was open for 1% of the time, Pallas kernels for 11%

profile of v1, /device:TPU:1, one launch (start us, length us, event | category | flops | bytes accessed | tf_op | source)
XLA Modules:
  0.0 144.8 jit_solution(14289930576996069853)
XLA Ops:
  0.7 1.2 copy-done.3
  2.5 1.8 %pack.1 = (bf16[512,896]{1,0:T(8,128)(2,1)}, s32[1,512]{1,0:T(1,128)S(1)}) custom-call(s32[1,512]{1,0:T(1,128)S(1)} %copy-done.5, bf16[512,768]{1,0:T(8,128)(2,1)S(1)} %bitcast.20), custom_call_target="tpu_custom_call" | custom-call | flops 800000000 | bytes 4000000 | tf_op jit(solution)/shard_map/pack/pallas_call | solution.py:342
  4.4 10.6 %all-to-all-start = ((bf16[32,16,896]{2,1,0:T(8,128)(2,1)}), bf16[32,16,896]{2,1,0:T(8,128)(2,1)S(1)}, u32[]{:S(2)}, u32[]{:S(2)}) async-start(bf16[32,16,896]{2,1,0:T(8,128)(2,1)} %bitcast.6), calls=%async_computation | async-start | bytes 1835008 | tf_op jit(solution)/shard_map/all_to_all | solution.py:328
  16.3 14.5 %all-to-all-done = bf16[32,16,896]{2,1,0:T(8,128)(2,1)S(1)} async-done(((bf16[32,16,896]{2,1,0:T(8,128)(2,1)}), bf16[32,16,896]{2,1,0:T(8,128)(2,1)S(1)}, u32[]{:S(2)}, u32[]{:S(2)}) %all-to-all-start) | async-done | bytes 917536 | tf_op jit(solution)/shard_map/all_to_all | solution.py:328
  30.8 1.5 %copy-done.1 = bf16[768,1152]{1,0:T(8,128)(2,1)S(1)} copy-done((bf16[768,1152]{1,0:T(8,128)(2,1)S(1)}, bf16[768,1152]{1,0:T(8,128)(2,1)}, u32[]{:S(2)}) %copy-start.1) | copy-done | bytes 1769496
  32.3 3.3 %project.1 = (bf16[512,1152]{1,0:T(8,128)(2,1)S(1)}, bf16[192,384]{1,0:T(8,128)(2,1)S(1)}, bf16[192,384]{1,0:T(8,128)(2,1)S(1)}, f32[192,384]{1,0:T(8,128)S(1)},...) custom-call(s32[5]{0:T(128)S(1)} %stack.19.scal_ref, bf16[512,896]{1,0:T(8,128)(2,1)S(1)} %bitcast.18, ...), custom_call_target="tpu_custom_call" | custom-call | flops 3000000000 | bytes 4000000 | tf_op jit(solution)/shard_map/project/pallas_call | solution.py:351
  35.6 1.0 copy-done.11
  36.7 16.4 %all_to_all.34.recv_ref = bf16[32,40,256]{2,1,0:T(8,128)(2,1)S(1)} all-to-all(bf16[32,40,256]{2,1,0:T(8,128)(2,1)S(1)} %get-tuple-element.19), channel_id=1, replica_groups=mesh['slide'=16,'ctx'=32] {'ctx'}, dimensions={0} | all-to-all | bytes 1310720 | tf_op jit(solution)/shard_map/all_to_all | solution.py:328
  53.0 3.2 %far.1 = bf16[32,40,256]{2,1,0:T(8,128)(2,1)} custom-call(s32[5]{0:T(128)S(1)} %stack.19.scal_ref, bf16[32,40,256]{2,1,0:T(8,128)(2,1)S(1)} %all_to_all.34.recv_ref), custom_call_target="tpu_custom_call" | custom-call | flops 3000000000 | bytes 4000000 | tf_op jit(solution)/shard_map/far/pallas_call | solution.py:380
  56.2 4.1 %all-to-all-start.2 = ((bf16[32,40,256]{2,1,0:T(8,128)(2,1)}), bf16[32,40,256]{2,1,0:T(8,128)(2,1)S(1)}, u32[]{:S(2)}, u32[]{:S(2)}) async-start(bf16[32,40,256]{2,1,0:T(8,128)(2,1)} %far.1), calls=%async_computation.2 | async-start | bytes 1310720 | tf_op jit(solution)/shard_map/all_to_all | solution.py:328
  60.4 1.3 copy-done.12
  61.6 8.7 %local_rows.1 = (bf16[512,384]{1,0:T(8,128)(2,1)S(1)}, bf16[512,384]{1,0:T(8,128)(2,1)S(1)}, f32[512,384]{1,0:T(8,128)S(1)}, f32[512,384]{1,0:T(8,128)S(1)}) custom-call(s32[5]{0:T(128)S(1)} %stack.19.scal_ref, bf16[512,1152]{1,0:T(8,128)(2,1)S(1)} %copy-done.12, bf16[512,1152]{1,0:T(8,128)(2,1)S(1)} %copy-done.12, bf16[512,1152]{1,0:T(8,128)(2,1)S(1)} %copy-done.12, ...), custom_call_target="tpu_custom_call" | custom-call | flops 12000000000 | bytes 4000000 | tf_op jit(solution)/shard_map/local_rows/pallas_call | solution.py:370
  71.1 0.9 copy-done.14
  71.9 0.9 copy-done.16
  72.8 0.8 copy-done.18
  73.6 1.0 copy-done.7
  74.6 1.0 copy-done.9
  75.5 2.9 %weight.1 = bf16[32,16,640]{2,1,0:T(8,128)(2,1)} custom-call(s32[5]{0:T(128)S(1)} %stack.19.scal_ref, bf16[32,40,256]{2,1,0:T(8,128)(2,1)S(1)} %all-to-all-done.2.recv_ref, f32[192,384]{1,0:T(8,128)S(1)} %copy-done.9, bf16[512,384]{1,0:T(8,128)(2,1)S(1)} %copy-done.7, bf16[512,768]{1,0:T(8,128)(2,1)S(1)} %bitcast.21), custom_call_target="tpu_custom_call" | custom-call | flops 1000000000 | bytes 4000000 | tf_op jit(solution)/shard_map/weight/pallas_call | solution.py:385
  78.4 7.7 %all-to-all-start.4 = ((bf16[32,16,640]{2,1,0:T(8,128)(2,1)}), bf16[32,16,640]{2,1,0:T(8,128)(2,1)}, u32[]{:S(2)}, u32[]{:S(2)}) async-start(bf16[32,16,640]{2,1,0:T(8,128)(2,1)} %weight.1), calls=%async_computation.4 | async-start | bytes 1310720 | tf_op jit(solution)/shard_map/all_to_all | solution.py:328
  86.2 1.5 %copy-done.2 = bf16[768,1152]{1,0:T(8,128)(2,1)S(1)} copy-done((bf16[768,1152]{1,0:T(8,128)(2,1)S(1)}, bf16[768,1152]{1,0:T(8,128)(2,1)}, u32[]{:S(2)}) %copy-start.2) | copy-done | bytes 1769496
  87.6 1.3 copy-done.13
  88.9 1.1 copy-done.17
  90.0 1.0 copy-done.19
  91.0 0.9 copy-done.21
  91.9 6.0 %finish.1 = (bf16[512,768]{1,0:T(8,128)(2,1)}, f32[2,192,64]{2,1,0:T(8,128)}) custom-call(s32[5]{0:T(128)S(1)} %stack.19.scal_ref, bf16[32,40,256]{2,1,0:T(8,128)(2,1)S(1)} %all-to-all-done.2.recv_ref, bf16[512,1152]{1,0:T(8,128)(2,1)S(1)} %copy-done.13, bf16[192,384]{1,0:T(8,128)(2,1)S(1)} %get-tuple-element.21.far_ref, bf16[192,384]{1,0:T(8,128)(2,1)S(1)} %copy-done.21, ...), custom_call_target="tpu_custom_call" | custom-call | flops 4000000000 | bytes 4000000 | tf_op jit(solution)/shard_map/finish/pallas_call | solution.py:398
  97.9 1.1 all-to-all-done.4
  99.1 6.3 %all-to-all-start.3 = ((bf16[32,16,768]{2,1,0:T(8,128)(2,1)}), bf16[32,16,768]{2,1,0:T(8,128)(2,1)S(1)}, u32[]{:S(2)}, u32[]{:S(2)}) async-start(bf16[32,16,768]{2,1,0:T(8,128)(2,1)} %bitcast.9), calls=%async_computation.3 | async-start | bytes 1572864 | tf_op jit(solution)/shard_map/all_to_all | solution.py:328
  105.3 1.2 convert_reduce_fusion
  107.2 12.4 %all-to-all-done.3 = bf16[32,16,768]{2,1,0:T(8,128)(2,1)S(1)} async-done(((bf16[32,16,768]{2,1,0:T(8,128)(2,1)}), bf16[32,16,768]{2,1,0:T(8,128)(2,1)S(1)}, u32[]{:S(2)}, u32[]{:S(2)}) %all-to-all-start.3) | async-done | bytes 786464 | tf_op jit(solution)/shard_map/all_to_all | solution.py:328
  119.6 13.0 %all-to-all-start.5 = ((f32[16,1,640]{2,1,0:T(1,128)}), f32[16,1,640]{2,1,0:T(1,128)S(1)}, u32[]{:S(2)}, u32[]{:S(2)}) async-start(f32[16,1,640]{2,1,0:T(1,128)} %all_to_all.26), calls=%async_computation.5 | async-start | bytes 81920 | tf_op jit(solution)/shard_map/all_to_all | solution.py:328
  132.6 1.5 %unpack.1 = bf16[512,768]{1,0:T(8,128)(2,1)} custom-call(s32[1,512]{1,0:T(1,128)S(1)} %get-tuple-element.17.slot_ref, bf16[512,768]{1,0:T(8,128)(2,1)S(1)} %bitcast.17), custom_call_target="tpu_custom_call" | custom-call | flops 400000000 | bytes 4000000 | tf_op jit(solution)/shard_map/unpack/pallas_call | solution.py:416
  134.1 10.0 %all-to-all-done.5 = f32[16,1,640]{2,1,0:T(1,128)S(1)} async-done(((f32[16,1,640]{2,1,0:T(1,128)}), f32[16,1,640]{2,1,0:T(1,128)S(1)}, u32[]{:S(2)}, u32[]{:S(2)}) %all-to-all-start.5) | async-done | bytes 40992 | tf_op jit(solution)/shard_map/all_to_all | solution.py:328
  (41 shorter events, 3.5 us)
Async XLA Ops:
  0.6 15.1 %copy-start = (bf16[384,768]{1,0:T(8,128)(2,1)S(1)}, bf16[384,768]{1,0:T(8,128)(2,1)}, u32[]{:S(2)}) copy-start(bf16[384,768]{1,0:T(8,128)(2,1)} %param.10) | copy-start | bytes 1769476
  0.6 1.2 copy-start.3
  1.8 0.7 copy-start.5
  4.4 11.4 %copy-start.4 = (bf16[1,512,768]{2,1,0:T(8,128)(2,1)S(1)}, bf16[1,512,768]{2,1,0:T(8,128)(2,1)}, u32[]{:S(2)}) copy-start(bf16[1,512,768]{2,1,0:T(8,128)(2,1)} %param.11) | copy-start | bytes 2359300
  4.4 26.5 %all-to-all-start = ((bf16[32,16,896]{2,1,0:T(8,128)(2,1)}), bf16[32,16,896]{2,1,0:T(8,128)(2,1)S(1)}, u32[]{:S(2)}, u32[]{:S(2)}) async-start(bf16[32,16,896]{2,1,0:T(8,128)(2,1)} %bitcast.6), calls=%async_computation | async-start | bytes 1835008 | tf_op jit(solution)/shard_map/all_to_all | solution.py:328
  30.8 1.5 %copy-start.1 = (bf16[768,1152]{1,0:T(8,128)(2,1)S(1)}, bf16[768,1152]{1,0:T(8,128)(2,1)}, u32[]{:S(2)}) copy-start(bf16[768,1152]{1,0:T(8,128)(2,1)} %weight_ref.3) | copy-start | bytes 5308420
  35.6 1.0 copy-start.11
  36.6 16.4 %copy-start.8 = (f32[192,384]{1,0:T(8,128)}, f32[192,384]{1,0:T(8,128)S(1)}, u32[]{:S(2)}) copy-start(f32[192,384]{1,0:T(8,128)S(1)} %get-tuple-element.23.mean_ref) | copy-start | bytes 884740
  36.6 19.6 %copy-start.20 = (bf16[192,384]{1,0:T(8,128)(2,1)}, bf16[192,384]{1,0:T(8,128)(2,1)S(1)}, u32[]{:S(2)}) copy-start(bf16[192,384]{1,0:T(8,128)(2,1)S(1)} %get-tuple-element.22.fgrad_ref) | copy-start | bytes 442372
  36.7 19.6 %copy-start.22 = (f32[192,128]{1,0:T(8,128)}, f32[192,128]{1,0:T(8,128)S(1)}, u32[]{:S(2)}) copy-start(f32[192,128]{1,0:T(8,128)S(1)} %get-tuple-element.24.lse_ref) | copy-start | bytes 294916
  56.2 17.4 %all-to-all-start.2 = ((bf16[32,40,256]{2,1,0:T(8,128)(2,1)}), bf16[32,40,256]{2,1,0:T(8,128)(2,1)S(1)}, u32[]{:S(2)}, u32[]{:S(2)}) async-start(bf16[32,40,256]{2,1,0:T(8,128)(2,1)} %far.1), calls=%async_computation.2 | async-start | bytes 1310720 | tf_op jit(solution)/shard_map/all_to_all | solution.py:328
  60.3 1.3 copy-start.12
  70.3 0.8 copy-start.6
  71.1 0.9 copy-start.14
  71.9 0.9 copy-start.16
  72.8 0.8 copy-start.18
  73.6 1.0 copy-start.7
  74.6 1.0 copy-start.9
  78.4 7.7 %copy-start.10 = (f32[192,384]{1,0:T(8,128)S(1)}, f32[192,384]{1,0:T(8,128)}, u32[]{:S(2)}) copy-start(f32[192,384]{1,0:T(8,128)} %copy-done.8) | copy-start | bytes 884740
  78.4 7.7 %copy-start.15 = (f32[512,384]{1,0:T(8,128)S(1)}, f32[512,384]{1,0:T(8,128)}, u32[]{:S(2)}) copy-start(f32[512,384]{1,0:T(8,128)} %copy-done.14) | copy-start | bytes 2359300
  78.4 7.7 %copy-start.23 = (f32[192,128]{1,0:T(8,128)S(1)}, f32[192,128]{1,0:T(8,128)}, u32[]{:S(2)}) copy-start(f32[192,128]{1,0:T(8,128)} %copy-done.22) | copy-start | bytes 294916
  78.4 20.6 %all-to-all-start.4 = ((bf16[32,16,640]{2,1,0:T(8,128)(2,1)}), bf16[32,16,640]{2,1,0:T(8,128)(2,1)}, u32[]{:S(2)}, u32[]{:S(2)}) async-start(bf16[32,16,640]{2,1,0:T(8,128)(2,1)} %weight.1), calls=%async_computation.4 | async-start | bytes 1310720 | tf_op jit(solution)/shard_map/all_to_all | solution.py:328
  86.1 1.5 %copy-start.2 = (bf16[768,1152]{1,0:T(8,128)(2,1)S(1)}, bf16[768,1152]{1,0:T(8,128)(2,1)}, u32[]{:S(2)}) copy-start(bf16[768,1152]{1,0:T(8,128)(2,1)} %weight_ref.3) | copy-start | bytes 5308420
  87.6 1.3 copy-start.13
  88.9 1.1 copy-start.17
  90.0 1.0 copy-start.19
  91.0 0.9 copy-start.21
  99.1 20.5 %all-to-all-start.3 = ((bf16[32,16,768]{2,1,0:T(8,128)(2,1)}), bf16[32,16,768]{2,1,0:T(8,128)(2,1)S(1)}, u32[]{:S(2)}, u32[]{:S(2)}) async-start(bf16[32,16,768]{2,1,0:T(8,128)(2,1)} %bitcast.9), calls=%async_computation.3 | async-start | bytes 1572864 | tf_op jit(solution)/shard_map/all_to_all | solution.py:328
  119.6 24.5 %all-to-all-start.5 = ((f32[16,1,640]{2,1,0:T(1,128)}), f32[16,1,640]{2,1,0:T(1,128)S(1)}, u32[]{:S(2)}, u32[]{:S(2)}) async-start(f32[16,1,640]{2,1,0:T(1,128)} %all_to_all.26), calls=%async_computation.5 | async-start | bytes 81920 | tf_op jit(solution)/shard_map/all_to_all | solution.py:328

commit v2 on v1

v2 whole, which is shorter than its diff:
```python
import math

import jax
import jax.numpy as jnp
from jax import lax
from jax.experimental import pallas as pl
from jax.experimental.pallas import tpu as pltpu
from jax.sharding import PartitionSpec as P

HD = 64
HEADS = 6
STRIDE = 16
PEERS = 32
ROWS = 512
PORTION = 16
GROUPS = ROWS // STRIDE
FAR = HEADS * GROUPS
WIDTH = 768
INNER = HEADS * HD
QUERIES = 8 * GROUPS
KEYS = PEERS * GROUPS
CHUNK = GROUPS + 8
PIECE = 640
ALL = 64 * 1024 * 1024
LIMIT = 48_000_000
PROJECT_LIMIT = 53_500_000
FLOOR = -1e30
SCALE = 0.125
LOG_SCALE = 0.125 * math.log2(math.e)
BF = jnp.bfloat16
F32 = jnp.float32


def nn(a, b):
    return lax.dot_general(a, b, (((1,), (0,)), ((), ())), preferred_element_type=F32)


def nt(a, b):
    return lax.dot_general(a, b, (((1,), (1,)), ((), ())), preferred_element_type=F32)


def tn(a, b):
    return lax.dot_general(a, b, (((0,), (0,)), ((), ())), preferred_element_type=F32)


def iota(shape, dim):
    return lax.broadcasted_iota(jnp.int32, shape, dim)


def mark(mask):
    return jnp.where(mask, 1.0, 0.0).astype(BF)


def split3(x):
    high = x.astype(BF)
    rest = x - high.astype(F32)
    middle = rest.astype(BF)
    low = (rest - middle.astype(F32)).astype(BF)
    return high.astype(F32), middle.astype(F32), low.astype(F32)


def key_bias(count, live):
    return jnp.where(iota((1, count), 1) < live, 0.0, FLOOR)


def far_rows():
    r = iota((FAR, ROWS), 0)
    return mark(((r & (GROUPS - 1)) * STRIDE + (r >> 5)) == iota((FAR, ROWS), 1))


def own_head():
    return (iota((FAR, INNER), 0) >> 5) == (iota((FAR, INNER), 1) >> 6)


def fold(offset):
    return mark((iota((INNER, 128), 0) & (HD - 1)) + offset == iota((INNER, 128), 1))


def pack_kernel(pos_ref, tiles_ref, send_ref, slot_ref):
    places = pos_ref[...]
    block = places >> 9
    member = iota((PEERS, ROWS), 0) == block
    before = mark(iota((ROWS, ROWS), 0) < iota((ROWS, ROWS), 1))
    counts = nn(mark(member), before)
    rank = jnp.sum(jnp.where(member, counts, 0.0), 0, keepdims=True)
    slot = block * PORTION + rank.astype(jnp.int32)
    slot_ref[...] = slot
    order = mark(iota((ROWS, ROWS), 0) == slot)
    send_ref[:, :WIDTH] = nn(order, tiles_ref[...]).astype(BF)
    inside = places & (ROWS - 1)
    line = iota((128, ROWS), 0)
    code = jnp.where(line == 0, inside >> 4, jnp.where(line == 1, inside & 15, 0))
    send_ref[:, WIDTH:] = nt(order, code.astype(F32).astype(BF)).astype(BF)


def project_kernel(
    scal_ref, recv_ref, weight_ref, grad_ref, send_ref, q_ref, kv_ref, code_ref, far_ref, fgrad_ref, mean_ref
):
    lane = iota((8, 128), 1)
    pick = jnp.where(iota((8, 128), 0) == 0, jnp.where(lane == 0, 16.0, jnp.where(lane == 1, 1.0, 0.0)), 0.0)
    code = recv_ref[:, WIDTH:]
    code_ref[...] = code
    code_ref.send()
    place = nt(pick.astype(BF), code)[0:1].astype(jnp.int32)
    order = mark(iota((ROWS, ROWS), 0) == place)
    sequence = nn(order, recv_ref[:, :WIDTH]).astype(BF)
    proj = nn(sequence, weight_ref[...]).astype(BF)
    q_ref[...] = proj[:, :INNER]
    kv_ref[...] = proj[:, INNER:]
    q_ref.send()
    kv_ref.send()
    chosen = far_rows()
    own = own_head()
    far = nn(chosen, proj)
    fq = jnp.where(own, far[:, :INNER], 0.0).astype(BF)
    fk = jnp.where(own, far[:, INNER : 2 * INNER], 0.0).astype(BF)
    fv = jnp.where(own, far[:, 2 * INNER :], 0.0).astype(BF)
    fgrad = jnp.where(own, nn(chosen, grad_ref[...]), 0.0).astype(BF)
    far_ref[...] = fq
    fgrad_ref[...] = fgrad
    far_ref.send()
    fgrad_ref.send()
    scores = nt(fq, proj[:, INNER : 2 * INNER]) * LOG_SCALE + key_bias(ROWS, scal_ref[0])
    top = jnp.max(scores, -1, keepdims=True)
    weight = jnp.exp2(scores - top)
    total = jnp.sum(weight, -1, keepdims=True)
    mean = jnp.where(own, nn(weight.astype(BF), proj[:, 2 * INNER :]) / total, 0.0)
    mean_ref[:, :INNER] = mean
    lse = top + jnp.log2(total)
    mean_ref[:, INNER:] = jnp.broadcast_to(lse, (FAR, 128))
    mean_ref.send()
    inner = jnp.sum(fgrad.astype(F32) * mean, -1, keepdims=True)
    first, second = fold(0), fold(HD)
    key_value = (nn(fk, first) + nn(fv, second)).astype(BF)
    query_grad = (nn(fq, first) + nn(fgrad, second)).astype(BF)
    column = iota((FAR, 128), 1)
    stats = jnp.zeros((FAR, 128), F32)
    for at, part in enumerate(split3(lse) + split3(inner)):
        stats = jnp.where(column == at, part, stats)
    stats = jnp.concatenate([stats, jnp.zeros((QUERIES - FAR, 128), F32)], 0).astype(BF)
    stats = nt(mark(iota((8, 128), 0) == iota((8, 128), 1)), stats).astype(BF)
    for peer in range(PEERS):
        head = (peer % 8) % HEADS
        rows = slice(head * GROUPS, (head + 1) * GROUPS)
        send_ref[peer, :GROUPS, :128] = key_value[rows]
        send_ref[peer, :GROUPS, 128:] = query_grad[rows]
        send_ref[peer, GROUPS:, :] = stats


def local_kernel(scal_ref, q_ref, kv_ref, grad_ref, att_ref, dq_ref, dk_ref, dv_ref):
    live = scal_ref[0]
    bias = key_bias(ROWS, live)
    row = iota((ROWS, 128), 0)
    side = iota((ROWS, 128), 1) >> 6
    zero = jnp.zeros((), BF)
    for pair in range(HEADS // 2):
        lanes = slice(pair * 128, pair * 128 + 128)
        q = q_ref[:, lanes]
        k = kv_ref[:, lanes]
        v = kv_ref[:, INNER + pair * 128 : INNER + pair * 128 + 128]
        grad = grad_ref[:, lanes]
        atts, dqs, dks, dvs = [], [], [], []
        for half in range(2):
            ours = side == half
            kept = ours & ((row & (STRIDE - 1)) != pair * 2 + half)
            query = jnp.where(ours, q, zero)
            out_grad = jnp.where(kept, grad, zero)
            scores = nt(query, k) * LOG_SCALE + bias
            weight = jnp.exp2(scores - jnp.max(scores, -1, keepdims=True))
            inverse = 1.0 / jnp.sum(weight, -1, keepdims=True)
            result = jnp.where(kept & (row < live), nn(weight.astype(BF), v) * inverse, 0.0)
            stat = jnp.sum(out_grad.astype(F32) * result, -1, keepdims=True)
            prob = weight * inverse
            dscore = (prob * (nt(out_grad, v) - stat) * SCALE).astype(BF)
            atts.append(result)
            dqs.append(jnp.where(kept, nn(dscore, k), 0.0))
            dks.append(tn(dscore, query))
            dvs.append(tn(prob.astype(BF), out_grad))
        att_ref[:, lanes] = (atts[0] + atts[1]).astype(BF)
        dq_ref[:, lanes] = (dqs[0] + dqs[1]).astype(BF)
        dk_ref[:, lanes] = dks[0] + dks[1]
        dv_ref[:, lanes] = dvs[0] + dvs[1]


def far_kernel(scal_ref, recv_ref, tie_ref, send_ref, lse_ref, stat_ref, share_ref, num_ref):
    first = scal_ref[2] * 8
    head = scal_ref[3]
    left = iota((QUERIES, 128), 1) < HD
    zero = jnp.zeros((), BF)
    pick = mark(iota((GROUPS, QUERIES), 1) == iota((GROUPS, QUERIES), 0) + head * GROUPS)
    kv = recv_ref[:, :GROUPS, :128].reshape(KEYS, 128)
    own_kv = recv_ref[pl.ds(first, 8), :GROUPS, :128].reshape(QUERIES, 128)
    last = scal_ref[1] - head
    bias = jnp.where(iota((1, KEYS), 1) * STRIDE < last, 0.0, FLOOR)
    own_bias = jnp.where((iota((1, QUERIES), 1) + first * GROUPS) * STRIDE < last, 0.0, FLOOR)
    key_out = jnp.zeros((QUERIES, 128), F32)
    value_out = jnp.zeros((QUERIES, 128), F32)
    for i in range(4):
        rows = slice(i * QUERIES, (i + 1) * QUERIES)
        mine = recv_ref[8 * i : 8 * i + 8, :GROUPS, 128:].reshape(QUERIES, 128)
        query = jnp.where(left, mine, zero)
        grad = jnp.where(left, zero, mine)
        parts = jnp.concatenate([nt(pick, recv_ref[8 * i + j, GROUPS:, :]) for j in range(8)], 0)
        lse = parts[:, 0:1] + parts[:, 1:2] + parts[:, 2:3]
        inner = parts[:, 3:4] + parts[:, 4:5] + parts[:, 5:6]
        scores = nt(query, kv) * LOG_SCALE + bias
        top = jnp.max(scores, -1, keepdims=True)
        weight = jnp.exp2(scores - top)
        ceiling = jnp.maximum(top, lse)
        gain = jnp.exp2(top - ceiling)
        near = jnp.exp2(lse - ceiling)
        total = jnp.sum(weight, -1, keepdims=True) * gain + near
        inverse = 1.0 / total
        share = near * inverse
        numerator = nn(weight.astype(BF), kv) * (gain * inverse)
        stat = jnp.sum(grad.astype(F32) * numerator, -1, keepdims=True) + share * inner
        lse = ceiling + jnp.log2(total)
        prob = jnp.exp2(nt(query, own_kv) * LOG_SCALE + own_bias - lse)
        dscore = (prob * (nt(grad, own_kv) - stat) * SCALE).astype(BF)
        key_out = key_out + tn(dscore, mine)
        value_out = value_out + tn(prob.astype(BF), mine)
        lse_ref[rows] = jnp.broadcast_to(lse, (QUERIES, 128))
        stat_ref[rows] = jnp.broadcast_to(stat, (QUERIES, 128))
        share_ref[rows] = jnp.broadcast_to(share, (QUERIES, 128))
        num_ref[rows] = numerator
    rows = pl.ds(pl.multiple_of(scal_ref[2] * QUERIES, QUERIES), QUERIES)
    mine = recv_ref[pl.ds(first, 8), :GROUPS, 128:].reshape(QUERIES, 128)
    query = jnp.where(left, mine, zero)
    grad = jnp.where(left, zero, mine)
    prob = jnp.exp2(nt(query, kv) * LOG_SCALE + bias - lse_ref[rows, 0:1])
    dscore = (prob * (nt(grad, kv) - stat_ref[rows, 0:1]) * SCALE).astype(BF)
    query_out = jnp.where(left, nn(dscore, kv), num_ref[rows]).astype(BF)
    key_out = jnp.where(left, key_out, value_out).astype(BF)
    column = iota((QUERIES, 128), 1)
    stats = jnp.zeros((QUERIES, 128), F32)
    for at, part in enumerate(split3(share_ref[rows])):
        stats = jnp.where(column == at, part, stats)
    stats = nt(mark(iota((8, 128), 0) == iota((8, 128), 1)), stats.astype(BF)).astype(BF)
    for j in range(8):
        send_ref[j, :GROUPS, :128] = key_out[j * GROUPS : (j + 1) * GROUPS]
        send_ref[j, :GROUPS, 128:] = query_out[j * GROUPS : (j + 1) * GROUPS]
        send_ref[j, GROUPS:, :] = stats


def returned_far(scal_ref, recv_ref):
    pick = mark(iota((GROUPS, QUERIES), 1) == iota((GROUPS, QUERIES), 0) + scal_ref[4] * GROUPS)
    shares = jnp.concatenate([nt(pick, recv_ref[h, GROUPS:, :]) for h in range(HEADS)], 0)
    share = shares[:, 0:1] + shares[:, 1:2] + shares[:, 2:3]
    query_out = recv_ref[:HEADS, :GROUPS, 128:].reshape(FAR, 128)
    return share, query_out


def far_result(scal_ref, share, query_out, mean):
    r = iota((FAR, INNER), 0)
    live = (r & (GROUPS - 1)) * STRIDE + (r >> 5) < scal_ref[0]
    numerator = nt(query_out, fold(HD))
    return jnp.where(live & own_head(), numerator + share * mean, 0.0)


def weight_pieces(result, att_ref, cot_ref, send_ref):
    attention = att_ref[...] + tn(far_rows(), result.astype(BF)).astype(BF)
    new = iota((INNER, INNER), 1)
    old = 3 * (8 * (new & 15) + ((new >> 4) & 7)) + (new >> 7)
    attention = nn(attention, mark(iota((INNER, INNER), 0) == old)).astype(BF)
    terms = (tn(attention, cot_ref[...]) * (1.0 / 512.0)).astype(BF)
    one, two, three = terms[:128], terms[128:256], terms[256:]
    pieces = (
        one[:, :PIECE],
        jnp.concatenate([one[:, 512:], two[:, :384]], 1),
        jnp.concatenate([two[:, 384:], three[:, :256]], 1),
        three[:, 128:],
    )
    for r in range(4):
        for q in range(8):
            send_ref[4 * q + r, :, WIDTH:] = pieces[r][16 * q : 16 * q + 16]


def finish_kernel(
    scal_ref,
    recv_ref,
    mean_ref,
    att_ref,
    cot_ref,
    far_ref,
    fgrad_ref,
    kv_ref,
    dk_ref,
    dv_ref,
    dq_ref,
    weight_ref,
    code_ref,
    send_ref,
    pair_ref,
):
    share, query_out = returned_far(scal_ref, recv_ref)
    result = far_result(scal_ref, share, query_out, mean_ref[:, :INNER])
    weight_pieces(result, att_ref, cot_ref, send_ref)
    fq, fgrad = far_ref[...], fgrad_ref[...]
    keys, values = kv_ref[:, :INNER], kv_ref[:, INNER:]
    stat = jnp.sum(fgrad.astype(F32) * result, -1, keepdims=True)
    scores = nt(fq, keys) * LOG_SCALE + key_bias(ROWS, scal_ref[0])
    prob = jnp.exp2(scores - mean_ref[:, INNER : INNER + 1]) * share
    dscore = (prob * (nt(fgrad, values) - stat) * SCALE).astype(BF)
    own = own_head()
    chosen = far_rows()
    far_dq = jnp.where(own, nn(dscore, keys) + nt(query_out, fold(0)), 0.0).astype(BF)
    pairs = recv_ref[:HEADS, :GROUPS, :128].reshape(FAR, 128)
    scaled = pairs.astype(F32) * 32.0
    pair_ref[0] = scaled[:, :HD]
    pair_ref[1] = scaled[:, HD:]
    far_dk = jnp.where(own, nt(pairs, fold(0)), 0.0).astype(BF)
    far_dv = jnp.where(own, nt(pairs, fold(HD)), 0.0).astype(BF)
    grad_query = dq_ref[...] + tn(chosen, far_dq).astype(BF)
    grad_key = (dk_ref[...] + tn(dscore, fq) + tn(chosen, far_dk)).astype(BF)
    grad_value = (dv_ref[...] + tn(prob.astype(BF), fgrad) + tn(chosen, far_dv)).astype(BF)
    rows = nt(grad_query, weight_ref[:, :INNER])
    rows = rows + nt(grad_key, weight_ref[:, INNER : 2 * INNER])
    rows = rows + nt(grad_value, weight_ref[:, 2 * INNER :])
    code = code_ref[...].astype(F32)
    place = (code[:, 0:1] * 16.0 + code[:, 1:2]).astype(jnp.int32)
    order = mark(iota((ROWS, ROWS), 1) == place)
    back = nn(order, rows.astype(BF)).astype(BF)
    for peer in range(PEERS):
        send_ref[peer, :, :WIDTH] = back[PORTION * peer : PORTION * (peer + 1)]


def pieces_kernel(scal_ref, got_ref, out_ref):
    total = got_ref[0, :, WIDTH:].astype(F32)
    for peer in range(1, PEERS):
        total = total + got_ref[peer, :, WIDTH:].astype(F32)
    turned = jnp.concatenate([total[:, HD:], total[:, :HD]], 1)
    total = jnp.where(scal_ref[5] == 1, turned, total)
    for k in range(PIECE // 128):
        out_ref[:, k, :] = total[:, k * 128 : (k + 1) * 128]
    out_ref[:, PIECE // 128 :, :] = jnp.zeros((16, 8 - PIECE // 128, 128), F32)


def unpack_kernel(slot_ref, rows_ref, out_ref):
    order = mark(iota((ROWS, ROWS), 0) == slot_ref[...])
    out_ref[...] = tn(order, rows_ref[:, :, :WIDTH].reshape(ROWS, WIDTH)).astype(BF)


class Late:
    def __init__(self, source, buffer, semaphore):
        self.buffer = buffer
        self.copy = pltpu.make_async_copy(source, buffer, semaphore)
        self.copy.start()
        self.ready = False

    def wait(self):
        if not self.ready:
            self.copy.wait()
            self.ready = True

    def __getitem__(self, index):
        self.wait()
        return self.buffer[index]


class Early:
    def __init__(self, target, buffer, semaphore):
        self.buffer = buffer
        self.copy = pltpu.make_async_copy(buffer, target, semaphore)
        self.sent = False

    def __setitem__(self, index, value):
        self.buffer[index] = value

    def send(self):
        if not self.sent:
            self.copy.start()
            self.sent = True


HERE, LATE, TIE, SCALAR = "here", "late", "tie", "scalar"
SPACES = {
    HERE: pl.BlockSpec(memory_space=pltpu.VMEM),
    TIE: pl.BlockSpec(memory_space=pl.ANY),
    SCALAR: pl.BlockSpec(memory_space=pltpu.SMEM),
}
FAR_AWAY = pl.BlockSpec(memory_space=pltpu.HBM)
QUERY = (0, ROWS, 0, INNER)
KEY_VALUE = (0, ROWS, INNER, 2 * INNER)
CODE = (0, ROWS, 3 * INNER, 128)
FAR_QUERY = (ROWS, FAR, 0, INNER)
FAR_GRAD = (ROWS, FAR, INNER, INNER)
MEAN = (0, FAR, 0, INNER + 128)
ATTENTION = (0, ROWS, 0, INNER)
GRAD_QUERY = (0, ROWS, INNER, INNER)
GRAD_KEY = (0, ROWS, 0, INNER)
GRAD_VALUE = (0, ROWS, INNER, INNER)
LEFT = ((6656, 3 * INNER + 128), BF, (QUERY, KEY_VALUE, CODE, FAR_QUERY, FAR_GRAD))
MEANS = ((8320, INNER + 128), F32, (MEAN,))
GRADS16 = ((11136, 2 * INNER), BF, (ATTENTION, GRAD_QUERY))
GRADS32 = ((5632, 2 * INNER), F32, (GRAD_KEY, GRAD_VALUE))


def part(ref, window):
    if window == LATE:
        return ref
    return ref.at[pl.ds(window[0], window[1]), pl.ds(window[2], window[3])]


def call(body, name, flops, ins, outs, scratch=(), limit=LIMIT):
    staged = []
    for array, kind in ins:
        if kind not in SPACES:
            staged.append((array.shape if kind == LATE else (kind[1], kind[3]), array.dtype))
    for dims, dtype, kind in outs:
        if kind == LATE:
            staged.append((dims, dtype))
        elif kind not in SPACES:
            staged += [((w[1], w[3]), dtype) for w in kind]

    def kernel(*refs):
        refs = list(refs)
        operands = [refs.pop(0) for _ in ins]
        targets = [refs.pop(0) for _ in outs]
        buffers = [refs.pop(0) for _ in staged]
        semaphores = refs.pop(0) if staged else None
        at = 0
        for i, (_, kind) in enumerate(ins):
            if kind not in SPACES:
                operands[i] = Late(part(operands[i], kind), buffers[at], semaphores.at[at])
                at += 1
        results = []
        for target, (_, _, kind) in zip(targets, outs):
            if kind in SPACES:
                results.append(target)
                continue
            for w in (LATE,) if kind == LATE else kind:
                results.append(Early(part(target, w), buffers[at], semaphores.at[at]))
                at += 1
        body(*operands, *results, *refs)
        for operand in operands:
            if isinstance(operand, Late):
                operand.wait()
        for result in results:
            if isinstance(result, Early):
                result.send()
        for result in results:
            if isinstance(result, Early):
                result.copy.wait()

    return pl.pallas_call(
        kernel,
        out_shape=[jax.ShapeDtypeStruct(dims, dtype) for dims, dtype, _ in outs],
        in_specs=[SPACES.get(kind, FAR_AWAY) for _, kind in ins],
        out_specs=[SPACES.get(kind, FAR_AWAY) for _, _, kind in outs],
        scratch_shapes=[pltpu.VMEM(dims, dtype) for dims, dtype in staged]
        + ([pltpu.SemaphoreType.DMA((len(staged),))] if staged else [])
        + list(scratch),
        name=name,
        compiler_params=pltpu.CompilerParams(vmem_limit_bytes=limit),
        cost_estimate=pl.CostEstimate(flops=flops, bytes_accessed=4_000_000, transcendentals=0),
    )(*[a for a, _ in ins])


def exchange(rows, axis):
    return lax.all_to_all(rows, axis, split_axis=0, concat_axis=0, tiled=True)


def local(tiles, tile_pos, lengths, qkv_weight, out_weight, cotangent):
    device = lax.axis_index("ctx")
    length = lengths[0]
    live = length - device * ROWS
    scal = jnp.stack([live, length, device // 8, (device % 8) % HEADS, device % 8, device % 2]).astype(jnp.int32)
    cot = cotangent[0]

    sent, slot = call(
        pack_kernel,
        "pack",
        800_000_000,
        [(tile_pos, LATE), (tiles[0], LATE)],
        [((ROWS, 896), BF, LATE), ((1, ROWS), jnp.int32, LATE)],
        limit=ALL,
    )
    got = exchange(sent.reshape(PEERS, PORTION, 896), "ctx").reshape(ROWS, 896)

    grad_attn = jnp.einsum("qd,cd->qc", cot, out_weight, preferred_element_type=F32).astype(BF)
    alive = lax.broadcasted_iota(jnp.int32, (ROWS, 1), 0) < live
    grad_out = jnp.where(alive, grad_attn, jnp.zeros((), BF))

    far_sent, left, means = call(
        project_kernel,
        "project",
        3_000_000_000,
        [(scal, SCALAR), (got, HERE), (qkv_weight, LATE), (grad_out, LATE)],
        [((PEERS, CHUNK, 256), BF, LATE), LEFT, MEANS],
        limit=PROJECT_LIMIT,
    )
    far_got = exchange(far_sent, "ctx")

    grads16, grads32 = call(
        local_kernel,
        "local_rows",
        12_000_000_000,
        [(scal, SCALAR), (left, QUERY), (left, KEY_VALUE), (grad_out, LATE)],
        [GRADS16, GRADS32],
    )

    (far_back,) = call(
        far_kernel,
        "far",
        6_000_000_000,
        [(scal, SCALAR), (far_got, HERE), (grads16, TIE)],
        [((8, CHUNK, 256), BF, HERE)],
        [pltpu.VMEM((KEYS, 128), F32)] * 4,
    )
    blocks = [[8 * b + j for j in range(8)] for b in range(PEERS // 8)]
    far_back = lax.all_to_all(
        far_back, "ctx", split_axis=0, concat_axis=0, axis_index_groups=blocks, tiled=True
    )

    back, pair = call(
        finish_kernel,
        "finish",
        4_000_000_000,
        [
            (scal, SCALAR),
            (far_back, HERE),
            (means, MEAN),
            (grads16, ATTENTION),
            (cot, LATE),
            (left, FAR_QUERY),
            (left, FAR_GRAD),
            (left, KEY_VALUE),
            (grads32, GRAD_KEY),
            (grads32, GRAD_VALUE),
            (grads16, GRAD_QUERY),
            (qkv_weight, LATE),
            (left, CODE),
        ],
        [((PEERS, PORTION, WIDTH + PIECE), BF, HERE), ((2, FAR, HD), F32, LATE)],
    )
    returned = exchange(back, "ctx")
    (pieces,) = call(
        pieces_kernel,
        "pieces",
        1_000_000,
        [(scal, SCALAR), (returned, HERE)],
        [((16, 8, 128), F32, HERE)],
    )
    pieces = exchange(pieces, "slide")
    weight_grad = jnp.sum(pieces, 0).reshape(-1)[:576]
    (tile_grads,) = call(
        unpack_kernel, "unpack", 400_000_000, [(slot, LATE), (returned, HERE)], [((ROWS, WIDTH), BF, LATE)]
    )
    return (tile_grads[None], weight_grad, pair.reshape(1, 2, HEADS, GROUPS, HD))


def solution(mesh):
    placed = (
        P("slide", "ctx", None),
        P("slide", "ctx"),
        P("slide"),
        P(),
        P(),
        P("slide", "ctx", None),
    )
    return jax.shard_map(
        local,
        mesh=mesh,
        in_specs=placed,
        out_specs=(
            P("slide", "ctx", None),
            P(("slide", "ctx")),
            P("slide", None, None, "ctx", None),
        ),
        check_vma=False,
    )
```

time: 146 us -> 127 us (0.87)
  local copies, waits for them, and re-layouts: 18.1 us -> 0.1 us
  blocking collectives: 16.4 us -> 34.4 us
  starting transfers between devices: 41.6 us -> 27.4 us
  waiting for transfers between devices: 38 us -> 26.3 us
  Pallas kernels: 27.4 us -> 34.8 us
    unnamed x48 -> x6, local copies, waits for them, and re-layouts: 16.7 us -> 0.02 us
    all_to_all x5 -> x3, starting transfers between devices: 41.6 us -> 27.4 us  [exchange(): return lax.all_to_all(rows, axis, split_axis=0, concat_axis=0, tiled=True)]
    all_to_all x5 -> x3, waiting for transfers between devices: 38 us -> 26.3 us  [exchange(): return lax.all_to_all(rows, axis, split_axis=0, concat_axis=0, tiled=True)]
    all_to_all x1, blocking collectives: 16.4 us -> 25.9 us  [exchange(): return lax.all_to_all(rows, axis, split_axis=0, concat_axis=0, tiled=True)]
    all_to_all x0 -> x1, blocking collectives: none -> 8.5 us  [local(): lax.all_to_all(far_back, 'ctx', split_axis=0, concat_axis=0, axis_index_g...]
    pallas_call x7, Pallas kernels: 27.4 us -> 34.8 us  [call(): pl.pallas_call(kernel, out_shape=[jax.ShapeDtypeStruct(dims, dtype) for d...]
  transfers between devices with their start and end apart: 5 -> 3, of which waited for: 4 -> 3; matrix products, arithmetic and copies ran while one was open for 1% -> 2% of each run, Pallas kernels for 11% -> 9%
where the time goes in v2:
time: 127 us
  Pallas kernels  34.8 us (27%)
  blocking collectives  34.4 us (27%)
  starting transfers between devices  27.4 us (22%)
  waiting for transfers between devices  26.3 us (21%)
  matrix products  1.9 us (1%)
  between operations  1.43 us (1%)
    pallas_call x7, Pallas kernels, call(): pl.pallas_call(kernel, out_shape=[jax.ShapeDtypeStruct(dims, dtype) for d...  34.8 us
    all_to_all x3, starting transfers between devices, exchange(): return lax.all_to_all(rows, axis, split_axis=0, concat_axis=0, tiled=True)  27.4 us
    all_to_all x3, waiting for transfers between devices, exchange(): return lax.all_to_all(rows, axis, split_axis=0, concat_axis=0, tiled=True)  26.3 us
    all_to_all x1, blocking collectives, exchange(): return lax.all_to_all(rows, axis, split_axis=0, concat_axis=0, tiled=True)  25.9 us
    all_to_all x1, blocking collectives, local(): lax.all_to_all(far_back, 'ctx', split_axis=0, concat_axis=0, axis_index_g...  8.5 us
  transfers between devices with their start and end apart: 3, of which 3 were waited for; matrix products, arithmetic and copies ran while one was open for 2% of the time, Pallas kernels for 9%

profile of v2, /device:TPU:1, one launch (start us, length us, event | category | flops | bytes accessed | tf_op | source)
XLA Modules:
  0.0 126.9 jit_solution(17187684942339331137)
XLA Ops:
  0.6 2.9 %pack.1 = (bf16[512,896]{1,0:T(8,128)(2,1)}, s32[1,512]{1,0:T(1,128)}) custom-call(s32[1,512]{1,0:T(1,128)} %refs_0_.1, bf16[512,768]{1,0:T(8,128)(2,1)} %bitcast.23), custom_call_target="tpu_custom_call" | custom-call | flops 800000000 | bytes 4000000 | tf_op jit(solution)/shard_map/pack/pallas_call | solution.py:445
  3.5 10.5 %all-to-all-start = ((bf16[32,16,896]{2,1,0:T(8,128)(2,1)}), bf16[32,16,896]{2,1,0:T(8,128)(2,1)S(1)}, u32[]{:S(2)}, u32[]{:S(2)}) async-start(bf16[32,16,896]{2,1,0:T(8,128)(2,1)} %bitcast.20), calls=%async_computation | async-start | bytes 1835008 | tf_op jit(solution)/shard_map/all_to_all | solution.py:460
  14.6 0.1 stack.23.refs_0_
  14.7 1.9 %fusion.refs_3_ = bf16[512,384]{1,0:T(8,128)(2,1)S(1)} fusion(bf16[384,768]{1,0:T(8,128)(2,1)} %param.10, pred[512]{0:T(512)(128)(4,1)S(1)} %iota_compare_fusion, bf16[1,512,768]{2,1,0:T(8,128)(2,1)} %param.11), kind=kOutput, calls=%fused_computation.1 | convolution fusion | flops 302383104 | bytes 1769984 | tf_op jit(solution)/shard_map/qd,cd->qc/dot_general | solution.py:480
  16.6 13.2 %all-to-all-done = bf16[32,16,896]{2,1,0:T(8,128)(2,1)S(1)} async-done(((bf16[32,16,896]{2,1,0:T(8,128)(2,1)}), bf16[32,16,896]{2,1,0:T(8,128)(2,1)S(1)}, u32[]{:S(2)}, u32[]{:S(2)}) %all-to-all-start) | async-done | bytes 917536 | tf_op jit(solution)/shard_map/all_to_all | solution.py:460
  29.8 5.7 %project.1 = (bf16[32,40,256]{2,1,0:T(8,128)(2,1)}, bf16[6656,1280]{1,0:T(8,128)(2,1)}, f32[8320,512]{1,0:T(8,128)}) custom-call(s32[6]{0:T(128)S(1)} %stack.23.refs_0_, bf16[512,896]{1,0:T(8,128)(2,1)S(1)} %bitcast.18, bf16[768,1152]{1,0:T(8,128)(2,1)} %refs_11_.1, bf16[512,384]{1,0:T(8,128)(2,1)S(1)} %fusion.refs_3_), custom_call_target="tpu_custom_call" | custom-call | flops 3000000000 | bytes 4000000 | tf_op jit(solution)/shard_map/project/pallas_call | solution.py:445
  35.5 4.0 %all-to-all-start.1 = ((bf16[32,40,256]{2,1,0:T(8,128)(2,1)}), bf16[32,40,256]{2,1,0:T(8,128)(2,1)S(1)}, u32[]{:S(2)}, u32[]{:S(2)}) async-start(bf16[32,40,256]{2,1,0:T(8,128)(2,1)} %get-tuple-element.14), calls=%async_computation.1 | async-start | bytes 1310720 | tf_op jit(solution)/shard_map/all_to_all | solution.py:460
  39.5 9.9 %local_rows.1 = (bf16[11136,768]{1,0:T(8,128)(2,1)}, f32[5632,768]{1,0:T(8,128)}) custom-call(s32[6]{0:T(128)S(1)} %stack.23.refs_0_, bf16[6656,1280]{1,0:T(8,128)(2,1)} %get-tuple-element.15.refs_1_.refs_2_.refs_5_.refs_6_.refs_7_.refs_12_, bf16[6656,1280]{1,0:T(8,128)(2,1)} %get-tuple-element.15.refs_1_.refs_2_.refs_5_.refs_6_.refs_7_.refs_12_, ...), custom_call_target="tpu_custom_call" | custom-call | flops 12000000000 | bytes 4000000 | tf_op jit(solution)/shard_map/local_rows/pallas_call | solution.py:445
  49.4 0.0 copy-start
  49.4 0.0 copy-start.1
  49.4 3.1 %all-to-all-done.1.refs_1_ = bf16[32,40,256]{2,1,0:T(8,128)(2,1)S(1)} async-done(((bf16[32,40,256]{2,1,0:T(8,128)(2,1)}), bf16[32,40,256]{2,1,0:T(8,128)(2,1)S(1)}, u32[]{:S(2)}, u32[]{:S(2)}) %all-to-all-start.1) | async-done | bytes 655392 | tf_op jit(solution)/shard_map/all_to_all | solution.py:460
  52.5 5.4 %far.1 = bf16[8,40,256]{2,1,0:T(8,128)(2,1)S(1)} custom-call(s32[6]{0:T(128)S(1)} %stack.23.refs_0_, bf16[32,40,256]{2,1,0:T(8,128)(2,1)S(1)} %all-to-all-done.1.refs_1_, bf16[11136,768]{1,0:T(8,128)(2,1)} %get-tuple-element.16.refs_2_.refs_3_.refs_10_), custom_call_target="tpu_custom_call" | custom-call | flops 6000000000 | bytes 4000000 | tf_op jit(solution)/shard_map/far/pallas_call | solution.py:445
  57.9 8.5 %all_to_all.25.refs_1_ = bf16[8,40,256]{2,1,0:T(8,128)(2,1)S(1)} all-to-all(bf16[8,40,256]{2,1,0:T(8,128)(2,1)S(1)} %far.1), channel_id=1, replica_groups={{0,1,2,3,4,5,6,7},{8,9,10,11,12,13,14,15},{16,17,18,19,20,21,22,23},{24..., dimensions={0} | all-to-all | bytes 327680 | tf_op jit(solution)/shard_map/all_to_all | solution.py:511
  66.4 0.0 copy-done
  66.4 0.0 copy-done.1
  66.4 0.0 copy-start.2
  66.4 8.1 %finish.1 = (bf16[32,16,1408]{2,1,0:T(8,128)(2,1)S(1)}, f32[2,192,64]{2,1,0:T(8,128)}) custom-call(s32[6]{0:T(128)S(1)} %stack.23.refs_0_, bf16[8,40,256]{2,1,0:T(8,128)(2,1)S(1)} %all_to_all.25.refs_1_, f32[8320,512]{1,0:T(8,128)} %get-tuple-element.17.refs_2_, bf16[11136,768]{1,0:T(8,128)(2,1)} %get-tuple-element.16.refs_2_.refs_3_.refs_10_, ...), custom_call_target="tpu_custom_call" | custom-call | flops 4000000000 | bytes 4000000 | tf_op jit(solution)/shard_map/finish/pallas_call | solution.py:445
  74.6 25.9 %all_to_all.26.refs_1_ = bf16[32,16,1408]{2,1,0:T(8,128)(2,1)S(1)} all-to-all(bf16[32,16,1408]{2,1,0:T(8,128)(2,1)S(1)} %get-tuple-element.19), channel_id=1, replica_groups=mesh['slide'=16,'ctx'=32] {'ctx'}, dimensions={0} | all-to-all | bytes 2883584 | tf_op jit(solution)/shard_map/all_to_all | solution.py:460
  100.4 1.3 %pieces.1 = f32[16,8,128]{2,1,0:T(8,128)} custom-call(s32[6]{0:T(128)S(1)} %stack.23.refs_0_, bf16[32,16,1408]{2,1,0:T(8,128)(2,1)S(1)} %all_to_all.26.refs_1_), custom_call_target="tpu_custom_call" | custom-call | flops 1000000 | bytes 4000000 | tf_op jit(solution)/shard_map/pieces/pallas_call | solution.py:445
  101.8 12.9 %all-to-all-start.4 = ((f32[16,8,128]{2,1,0:T(8,128)}), f32[16,8,128]{2,1,0:T(8,128)S(1)}, u32[]{:S(2)}, u32[]{:S(2)}) async-start(f32[16,8,128]{2,1,0:T(8,128)} %pieces.1), calls=%async_computation.4 | async-start | bytes 131072 | tf_op jit(solution)/shard_map/all_to_all | solution.py:460
  114.7 0.0 copy-done.2
  114.7 1.5 %unpack.1 = bf16[512,768]{1,0:T(8,128)(2,1)} custom-call(s32[1,512]{1,0:T(1,128)S(1)} %copy-done.2, bf16[32,16,1408]{2,1,0:T(8,128)(2,1)S(1)} %all_to_all.26.refs_1_), custom_call_target="tpu_custom_call" | custom-call | flops 400000000 | bytes 4000000 | tf_op jit(solution)/shard_map/unpack/pallas_call | solution.py:445
  116.3 10.0 %all-to-all-done.4 = f32[16,8,128]{2,1,0:T(8,128)S(1)} async-done(((f32[16,8,128]{2,1,0:T(8,128)}), f32[16,8,128]{2,1,0:T(8,128)S(1)}, u32[]{:S(2)}, u32[]{:S(2)}) %all-to-all-start.4) | async-done | bytes 65568 | tf_op jit(solution)/shard_map/all_to_all | solution.py:460
  126.3 0.6 reduce_sum.9
  (1 shorter events, 0.0 us)
Async XLA Ops:
  3.5 26.3 %all-to-all-start = ((bf16[32,16,896]{2,1,0:T(8,128)(2,1)}), bf16[32,16,896]{2,1,0:T(8,128)(2,1)S(1)}, u32[]{:S(2)}, u32[]{:S(2)}) async-start(bf16[32,16,896]{2,1,0:T(8,128)(2,1)} %bitcast.20), calls=%async_computation | async-start | bytes 1835008 | tf_op jit(solution)/shard_map/all_to_all | solution.py:460
  35.5 17.0 %all-to-all-start.1 = ((bf16[32,40,256]{2,1,0:T(8,128)(2,1)}), bf16[32,40,256]{2,1,0:T(8,128)(2,1)S(1)}, u32[]{:S(2)}, u32[]{:S(2)}) async-start(bf16[32,40,256]{2,1,0:T(8,128)(2,1)} %get-tuple-element.14), calls=%async_computation.1 | async-start | bytes 1310720 | tf_op jit(solution)/shard_map/all_to_all | solution.py:460
  49.4 17.0 %copy-start = (bf16[768,1152]{1,0:T(8,128)(2,1)S(1)}, bf16[768,1152]{1,0:T(8,128)(2,1)}, u32[]{:S(2)}) copy-start(bf16[768,1152]{1,0:T(8,128)(2,1)} %refs_11_.1) | copy-start | bytes 5308420
  49.4 17.0 %copy-start.1 = (bf16[1,512,768]{2,1,0:T(8,128)(2,1)S(1)}, bf16[1,512,768]{2,1,0:T(8,128)(2,1)}, u32[]{:S(2)}) copy-start(bf16[1,512,768]{2,1,0:T(8,128)(2,1)} %param.11) | copy-start | bytes 2359300
  66.4 48.3 %copy-start.2 = (s32[1,512]{1,0:T(1,128)S(1)}, s32[1,512]{1,0:T(1,128)}, u32[]{:S(2)}) copy-start(s32[1,512]{1,0:T(1,128)} %get-tuple-element.12.refs_0_) | copy-start | bytes 6148
  101.8 24.5 %all-to-all-start.4 = ((f32[16,8,128]{2,1,0:T(8,128)}), f32[16,8,128]{2,1,0:T(8,128)S(1)}, u32[]{:S(2)}, u32[]{:S(2)}) async-start(f32[16,8,128]{2,1,0:T(8,128)} %pieces.1), calls=%async_computation.4 | async-start | bytes 131072 | tf_op jit(solution)/shard_map/all_to_all | solution.py:460

commit v3 on v2

--- a/solution.py
+++ b/solution.py
@@ -91,6 +91,11 @@
     line = iota((128, ROWS), 0)
     code = jnp.where(line == 0, inside >> 4, jnp.where(line == 1, inside & 15, 0))
     send_ref[:, WIDTH:] = nt(order, code.astype(F32).astype(BF)).astype(BF)
+
+
+def grad_kernel(scal_ref, cot_ref, weight_ref, out_ref):
+    grad = nt(cot_ref[...], weight_ref[...]).astype(BF)
+    out_ref[...] = jnp.where(iota((ROWS, INNER), 0) < scal_ref[0], grad, jnp.zeros((), BF))
 
 
 def project_kernel(
@@ -147,7 +152,34 @@
         send_ref[peer, GROUPS:, :] = stats
 
 
-def local_kernel(scal_ref, q_ref, kv_ref, grad_ref, att_ref, dq_ref, dk_ref, dv_ref):
+def local_kernel(
+    scal_ref,
+    q_ref,
+    kv_ref,
+    grad_ref,
+    code_ref,
+    far_ref,
+    fgrad_ref,
+    mean_ref,
+    kv_out,
+    code_out,
+    far_out,
+    fgrad_out,
+    mean_out,
+    att_ref,
+    dq_ref,
+    dk_ref,
+    dv_ref,
+):
+    for held, out in (
+        (kv_ref, kv_out),
+        (code_ref, code_out),
+        (far_ref, far_out),
+        (fgrad_ref, fgrad_out),
+        (mean_ref, mean_out),
+    ):
+        out[...] = held[...]
+        out.send()
     live = scal_ref[0]
     bias = key_bias(ROWS, live)
     row = iota((ROWS, 128), 0)
@@ -385,20 +417,23 @@
 FAR_QUERY = (ROWS, FAR, 0, INNER)
 FAR_GRAD = (ROWS, FAR, INNER, INNER)
 MEAN = (0, FAR, 0, INNER + 128)
-ATTENTION = (0, ROWS, 0, INNER)
-GRAD_QUERY = (0, ROWS, INNER, INNER)
-GRAD_KEY = (0, ROWS, 0, INNER)
-GRAD_VALUE = (0, ROWS, INNER, INNER)
 LEFT = ((6656, 3 * INNER + 128), BF, (QUERY, KEY_VALUE, CODE, FAR_QUERY, FAR_GRAD))
+GRADS = ((21504, INNER), BF, (QUERY,))
 MEANS = ((8320, INNER + 128), F32, (MEAN,))
-GRADS16 = ((11136, 2 * INNER), BF, (ATTENTION, GRAD_QUERY))
-GRADS32 = ((5632, 2 * INNER), F32, (GRAD_KEY, GRAD_VALUE))
 
 
 def part(ref, window):
     if window == LATE:
         return ref
     return ref.at[pl.ds(window[0], window[1]), pl.ds(window[2], window[3])]
+
+
+def scalars(lengths_ref):
+    device = lax.axis_index("ctx")
+    inner = device & 7
+    length = lengths_ref[0]
+    head = jnp.where(inner >= HEADS, inner - HEADS, inner)
+    return (length - device * ROWS, length, device >> 3, head, inner, device & 1)
 
 
 def call(body, name, flops, ins, outs, scratch=(), limit=LIMIT):
@@ -420,6 +455,8 @@
         semaphores = refs.pop(0) if staged else None
         at = 0
         for i, (_, kind) in enumerate(ins):
+            if kind == SCALAR:
+                operands[i] = scalars(operands[i])
             if kind not in SPACES:
                 operands[i] = Late(part(operands[i], kind), buffers[at], semaphores.at[at])
                 at += 1
@@ -461,10 +498,6 @@
 
 
 def local(tiles, tile_pos, lengths, qkv_weight, out_weight, cotangent):
-    device = lax.axis_index("ctx")
-    length = lengths[0]
-    live = length - device * ROWS
-    scal = jnp.stack([live, length, device // 8, (device % 8) % HEADS, device % 8, device % 2]).astype(jnp.int32)
     cot = cotangent[0]
 
     sent, slot = call(
@@ -477,33 +510,58 @@
     )
     got = exchange(sent.reshape(PEERS, PORTION, 896), "ctx").reshape(ROWS, 896)
 
-    grad_attn = jnp.einsum("qd,cd->qc", cot, out_weight, preferred_element_type=F32).astype(BF)
-    alive = lax.broadcasted_iota(jnp.int32, (ROWS, 1), 0) < live
-    grad_out = jnp.where(alive, grad_attn, jnp.zeros((), BF))
+    (grad_out,) = call(
+        grad_kernel,
+        "grad",
+        400_000_000,
+        [(lengths, SCALAR), (cot, LATE), (out_weight, LATE)],
+        [GRADS],
+    )
 
     far_sent, left, means = call(
         project_kernel,
         "project",
         3_000_000_000,
-        [(scal, SCALAR), (got, HERE), (qkv_weight, LATE), (grad_out, LATE)],
+        [(lengths, SCALAR), (got, HERE), (qkv_weight, LATE), (grad_out, QUERY)],
         [((PEERS, CHUNK, 256), BF, LATE), LEFT, MEANS],
         limit=PROJECT_LIMIT,
     )
     far_got = exchange(far_sent, "ctx")
 
-    grads16, grads32 = call(
+    key_value, code, far_q, far_grad, mean, att, dq, dk, dv, after = call(
         local_kernel,
         "local_rows",
         12_000_000_000,
-        [(scal, SCALAR), (left, QUERY), (left, KEY_VALUE), (grad_out, LATE)],
-        [GRADS16, GRADS32],
+        [
+            (lengths, SCALAR),
+            (left, QUERY),
+            (left, KEY_VALUE),
+            (grad_out, QUERY),
+            (left, CODE),
+            (left, FAR_QUERY),
+            (left, FAR_GRAD),
+            (means, MEAN),
+        ],
+        [
+            ((ROWS, 2 * INNER), BF, LATE),
+            ((ROWS, 128), BF, LATE),
+            ((FAR, INNER), BF, LATE),
+            ((FAR, INNER), BF, LATE),
+            ((FAR, INNER + 128), F32, LATE),
+            ((ROWS, INNER), BF, LATE),
+            ((ROWS, INNER), BF, LATE),
+            ((ROWS, INNER), F32, LATE),
+            ((ROWS, INNER), F32, LATE),
+            ((8320, 512), F32, ()),
+        ],
+        limit=ALL,
     )
 
     (far_back,) = call(
         far_kernel,
         "far",
         6_000_000_000,
-        [(scal, SCALAR), (far_got, HERE), (grads16, TIE)],
+        [(lengths, SCALAR), (far_got, HERE), (after, TIE)],
         [((8, CHUNK, 256), BF, HERE)],
         [pltpu.VMEM((KEYS, 128), F32)] * 4,
     )
@@ -517,19 +575,19 @@
         "finish",
         4_000_000_000,
         [
-            (scal, SCALAR),
+            (lengths, SCALAR),
             (far_back, HERE),
-            (means, MEAN),
-            (grads16, ATTENTION),
-            (cot, LATE),
-            (left, FAR_QUERY),
-            (left, FAR_GRAD),
-            (left, KEY_VALUE),
-            (grads32, GRAD_KEY),
-            (grads32, GRAD_VALUE),
-            (grads16, GRAD_QUERY),
-            (qkv_weight, LATE),
-            (left, CODE),
+            (mean, HERE),
+            (att, HERE),
+            (cot, HERE),
+            (far_q, HERE),
+            (far_grad, HERE),
+            (key_value, HERE),
+            (dk, HERE),
+            (dv, HERE),
+            (dq, HERE),
+            (qkv_weight, HERE),
+            (code, HERE),
         ],
         [((PEERS, PORTION, WIDTH + PIECE), BF, HERE), ((2, FAR, HD), F32, LATE)],
     )
@@ -538,7 +596,7 @@
         pieces_kernel,
         "pieces",
         1_000_000,
-        [(scal, SCALAR), (returned, HERE)],
+        [(lengths, SCALAR), (returned, HERE)],
         [((16, 8, 128), F32, HERE)],
     )
     pieces = exchange(pieces, "slide")

time: 127 us -> 125 us (0.984)
  local copies, waits for them, and re-layouts: 0.1 us -> 2.25 us
  matrix products: 1.9 us -> 0 us
  waiting for transfers between devices: 26.3 us -> 24.6 us
  Pallas kernels: 34.8 us -> 33.4 us
    unnamed x6 -> x28, local copies, waits for them, and re-layouts: 0.02 us -> 2.25 us
    dot_general x1 -> x0, matrix products: 1.9 us -> none  [local(): jnp.einsum('qd,cd->qc', cot, out_weight, preferred_element_type=F32)]
    all_to_all x3, waiting for transfers between devices: 26.3 us -> 24.6 us  [exchange(): return lax.all_to_all(rows, axis, split_axis=0, concat_axis=0, tiled=True)]
    pallas_call x7 -> x8, Pallas kernels: 34.8 us -> 33.4 us  [call(): pl.pallas_call(kernel, out_shape=[jax.ShapeDtypeStruct(dims, dtype) for d...]
  transfers between devices with their start and end apart: 3 -> 3, of which waited for: 3 -> 3; matrix products, arithmetic and copies ran while one was open for 2% -> 0% of each run, Pallas kernels for 9% -> 10%
where the time goes in v3:
time: 125 us
  blocking collectives  34.4 us (28%)
  Pallas kernels  33.4 us (27%)
  starting transfers between devices  28 us (22%)
  waiting for transfers between devices  24.6 us (20%)
  local copies, waits for them, and re-layouts  2.25 us (2%)
  between operations  1.51 us (1%)
    pallas_call x8, Pallas kernels, call(): pl.pallas_call(kernel, out_shape=[jax.ShapeDtypeStruct(dims, dtype) for d...  33.4 us
    all_to_all x3, starting transfers between devices, exchange(): return lax.all_to_all(rows, axis, split_axis=0, concat_axis=0, tiled=True)  28 us
    all_to_all x1, blocking collectives, exchange(): return lax.all_to_all(rows, axis, split_axis=0, concat_axis=0, tiled=True)  25.9 us
    all_to_all x3, waiting for transfers between devices, exchange(): return lax.all_to_all(rows, axis, split_axis=0, concat_axis=0, tiled=True)  24.6 us
    all_to_all x1, blocking collectives, local(): lax.all_to_all(far_back, 'ctx', split_axis=0, concat_axis=0, axis_index_g...  8.51 us
  transfers between devices with their start and end apart: 3, of which 3 were waited for; matrix products, arithmetic and copies ran while one was open for 0% of the time, Pallas kernels for 10%

profile of v3, /device:TPU:1, one launch (start us, length us, event | category | flops | bytes accessed | tf_op | source)
XLA Modules:
  0.0 124.8 jit_solution(6963117512092277715)
XLA Ops:
  0.6 2.9 %pack.1 = (bf16[512,896]{1,0:T(8,128)(2,1)}, s32[1,512]{1,0:T(1,128)}) custom-call(s32[1,512]{1,0:T(1,128)} %refs_0_.7, bf16[512,768]{1,0:T(8,128)(2,1)} %bitcast.14), custom_call_target="tpu_custom_call" | custom-call | flops 800000000 | bytes 4000000 | tf_op jit(solution)/shard_map/pack/pallas_call | solution.py:482
  3.5 10.5 %all-to-all-start = ((bf16[32,16,896]{2,1,0:T(8,128)(2,1)}), bf16[32,16,896]{2,1,0:T(8,128)(2,1)S(1)}, u32[]{:S(2)}, u32[]{:S(2)}) async-start(bf16[32,16,896]{2,1,0:T(8,128)(2,1)} %bitcast.11), calls=%async_computation | async-start | bytes 1835008 | tf_op jit(solution)/shard_map/all_to_all | solution.py:497
  14.6 0.0 copy-start.1
  14.6 1.1 copy-done.1
  15.7 1.1 copy-done.3
  16.8 1.6 %grad.1.refs_3_ = bf16[21504,384]{1,0:T(8,128)(2,1)} custom-call(s32[1]{0:T(128)S(6)} %copy.9.refs_0_, bf16[512,768]{1,0:T(8,128)(2,1)S(1)} %bitcast.9, bf16[384,768]{1,0:T(8,128)(2,1)S(1)} %copy-done.3), custom_call_target="tpu_custom_call" | custom-call | flops 400000000 | bytes 4000000 | tf_op jit(solution)/shard_map/grad/pallas_call | solution.py:482
  18.4 11.4 %all-to-all-done = bf16[32,16,896]{2,1,0:T(8,128)(2,1)S(1)} async-done(((bf16[32,16,896]{2,1,0:T(8,128)(2,1)}), bf16[32,16,896]{2,1,0:T(8,128)(2,1)S(1)}, u32[]{:S(2)}, u32[]{:S(2)}) %all-to-all-start) | async-done | bytes 917536 | tf_op jit(solution)/shard_map/all_to_all | solution.py:497
  29.8 5.2 %project.1 = (bf16[32,40,256]{2,1,0:T(8,128)(2,1)}, bf16[6656,1280]{1,0:T(8,128)(2,1)}, f32[8320,512]{1,0:T(8,128)}) custom-call(s32[1]{0:T(128)S(6)} %copy.9.refs_0_, bf16[512,896]{1,0:T(8,128)(2,1)S(1)} %bitcast.8, bf16[768,1152]{1,0:T(8,128)(2,1)} %refs_11_.1, bf16[21504,384]{1,0:T(8,128)(2,1)} %grad.1.refs_3_), custom_call_target="tpu_custom_call" | custom-call | flops 3000000000 | bytes 4000000 | tf_op jit(solution)/shard_map/project/pallas_call | solution.py:482
  35.0 4.6 %all-to-all-start.1 = ((bf16[32,40,256]{2,1,0:T(8,128)(2,1)}), bf16[32,40,256]{2,1,0:T(8,128)(2,1)}, u32[]{:S(2)}, u32[]{:S(2)}) async-start(bf16[32,40,256]{2,1,0:T(8,128)(2,1)} %get-tuple-element.22), calls=%async_computation.1 | async-start | bytes 1310720 | tf_op jit(solution)/shard_map/all_to_all | solution.py:497
  39.7 9.9 %local_rows.1 = (bf16[512,768]{1,0:T(8,128)(2,1)}, bf16[512,128]{1,0:T(8,128)(2,1)}, bf16[192,384]{1,0:T(8,128)(2,1)}, bf16[192,384]{1,0:T(8,128)(2,1)}, f32[192...) custom-call(s32[1]{0:T(128)S(6)} %copy.9.refs_0_, ...), custom_call_target="tpu_custom_call" | custom-call | flops 12000000000 | bytes 4000000 | tf_op jit(solution)/shard_map/local_rows/pallas_call | solution.py:482
  49.6 0.0 copy-start
  49.6 0.0 copy-start.2
  49.6 0.0 copy-start.5
  49.6 0.0 copy-start.11
  49.6 3.1 %all-to-all-done.1.refs_1_ = bf16[32,40,256]{2,1,0:T(8,128)(2,1)} async-done(((bf16[32,40,256]{2,1,0:T(8,128)(2,1)}), bf16[32,40,256]{2,1,0:T(8,128)(2,1)}, u32[]{:S(2)}, u32[]{:S(2)}) %all-to-all-start.1) | async-done | bytes 655392 | tf_op jit(solution)/shard_map/all_to_all | solution.py:497
  52.8 0.0 copy-start.4
  52.8 6.1 %far.1 = bf16[8,40,256]{2,1,0:T(8,128)(2,1)S(1)} custom-call(s32[1]{0:T(128)S(6)} %copy.9.refs_0_, bf16[32,40,256]{2,1,0:T(8,128)(2,1)} %all-to-all-done.1.refs_1_, f32[8320,512]{1,0:T(8,128)} %get-tuple-element.25.refs_2_), custom_call_target="tpu_custom_call" | custom-call | flops 6000000000 | bytes 4000000 | tf_op jit(solution)/shard_map/far/pallas_call | solution.py:482
  58.9 8.5 %all_to_all.25.refs_1_ = bf16[8,40,256]{2,1,0:T(8,128)(2,1)S(1)} all-to-all(bf16[8,40,256]{2,1,0:T(8,128)(2,1)S(1)} %far.1), channel_id=1, replica_groups={{0,1,2,3,4,5,6,7},{8,9,10,11,12,13,14,15},{16,17,18,19,20,21,22,23},{24..., dimensions={0} | all-to-all | bytes 327680 | tf_op jit(solution)/shard_map/all_to_all | solution.py:569
  67.4 0.0 copy-done.11
  67.4 0.0 copy-done.6
  67.4 0.0 copy-done.7
  67.4 0.0 copy-done.8
  67.4 0.0 copy-done.9
  67.5 0.0 copy-done.10
  67.5 0.0 copy-done.12
  67.5 5.5 %finish.1 = (bf16[32,16,1408]{2,1,0:T(8,128)(2,1)S(1)}, f32[2,192,64]{2,1,0:T(8,128)}) custom-call(s32[1]{0:T(128)S(6)} %copy.9.refs_0_, bf16[8,40,256]{2,1,0:T(8,128)(2,1)S(1)} %all_to_all.25.refs_1_, f32[192,512]{1,0:T(8,128)S(1)} %copy-done.8, bf16[512,384]{1,0:T(8,128)(2,1)S(1)} %copy-done.9, bf16[512,768]{1,0:T(8,128)(2,1)S(1)} %bitcast.10, ...), custom_call_target="tpu_custom_call" | custom-call | flops 4000000000 | bytes 4000000 | tf_op jit(solution)/shard_map/finish/pallas_call | solution.py:482
  73.0 25.9 %all_to_all.26.refs_1_ = bf16[32,16,1408]{2,1,0:T(8,128)(2,1)S(1)} all-to-all(bf16[32,16,1408]{2,1,0:T(8,128)(2,1)S(1)} %get-tuple-element.35), channel_id=1, replica_groups=mesh['slide'=16,'ctx'=32] {'ctx'}, dimensions={0} | all-to-all | bytes 2883584 | tf_op jit(solution)/shard_map/all_to_all | solution.py:497
  98.9 0.8 pieces.1
  99.7 12.9 %all-to-all-start.4 = ((f32[16,8,128]{2,1,0:T(8,128)}), f32[16,8,128]{2,1,0:T(8,128)S(1)}, u32[]{:S(2)}, u32[]{:S(2)}) async-start(f32[16,8,128]{2,1,0:T(8,128)} %pieces.1), calls=%async_computation.4 | async-start | bytes 131072 | tf_op jit(solution)/shard_map/all_to_all | solution.py:497
  112.6 1.5 %unpack.1 = bf16[512,768]{1,0:T(8,128)(2,1)} custom-call(s32[1,512]{1,0:T(1,128)S(1)} %copy-done.4, bf16[32,16,1408]{2,1,0:T(8,128)(2,1)S(1)} %all_to_all.26.refs_1_), custom_call_target="tpu_custom_call" | custom-call | flops 400000000 | bytes 4000000 | tf_op jit(solution)/shard_map/unpack/pallas_call | solution.py:482
  114.2 10.0 %all-to-all-done.4 = f32[16,8,128]{2,1,0:T(8,128)S(1)} async-done(((f32[16,8,128]{2,1,0:T(8,128)}), f32[16,8,128]{2,1,0:T(8,128)S(1)}, u32[]{:S(2)}, u32[]{:S(2)}) %all-to-all-start.4) | async-done | bytes 65568 | tf_op jit(solution)/shard_map/all_to_all | solution.py:497
  124.2 0.6 reduce_sum.9
  (13 shorter events, 0.0 us)
Async XLA Ops:
  3.5 26.3 %all-to-all-start = ((bf16[32,16,896]{2,1,0:T(8,128)(2,1)}), bf16[32,16,896]{2,1,0:T(8,128)(2,1)S(1)}, u32[]{:S(2)}, u32[]{:S(2)}) async-start(bf16[32,16,896]{2,1,0:T(8,128)(2,1)} %bitcast.11), calls=%async_computation | async-start | bytes 1835008 | tf_op jit(solution)/shard_map/all_to_all | solution.py:497
  14.6 1.1 copy-start.1
  15.7 1.1 copy-start.3
  35.0 17.7 %all-to-all-start.1 = ((bf16[32,40,256]{2,1,0:T(8,128)(2,1)}), bf16[32,40,256]{2,1,0:T(8,128)(2,1)}, u32[]{:S(2)}, u32[]{:S(2)}) async-start(bf16[32,40,256]{2,1,0:T(8,128)(2,1)} %get-tuple-element.22), calls=%async_computation.1 | async-start | bytes 1310720 | tf_op jit(solution)/shard_map/all_to_all | solution.py:497
  49.6 17.8 %copy-start = (bf16[768,1152]{1,0:T(8,128)(2,1)S(1)}, bf16[768,1152]{1,0:T(8,128)(2,1)}, u32[]{:S(2)}) copy-start(bf16[768,1152]{1,0:T(8,128)(2,1)} %refs_11_.1) | copy-start | bytes 5308420
  49.6 17.8 %copy-start.2 = (bf16[1,512,768]{2,1,0:T(8,128)(2,1)S(1)}, bf16[1,512,768]{2,1,0:T(8,128)(2,1)}, u32[]{:S(2)}) copy-start(bf16[1,512,768]{2,1,0:T(8,128)(2,1)} %param.11) | copy-start | bytes 2359300
  49.6 17.8 %copy-start.5 = (bf16[512,768]{1,0:T(8,128)(2,1)S(1)}, bf16[512,768]{1,0:T(8,128)(2,1)}, u32[]{:S(2)}) copy-start(bf16[512,768]{1,0:T(8,128)(2,1)} %get-tuple-element.30.refs_7_) | copy-start | bytes 2359300
  49.6 17.8 %copy-start.11 = (bf16[192,384]{1,0:T(8,128)(2,1)S(1)}, bf16[192,384]{1,0:T(8,128)(2,1)}, u32[]{:S(2)}) copy-start(bf16[192,384]{1,0:T(8,128)(2,1)} %get-tuple-element.28.refs_5_) | copy-start | bytes 442372
  52.8 14.7 %copy-start.6 = (f32[512,384]{1,0:T(8,128)S(1)}, f32[512,384]{1,0:T(8,128)}, u32[]{:S(2)}) copy-start(f32[512,384]{1,0:T(8,128)} %get-tuple-element.31.refs_8_) | copy-start | bytes 2359300
  52.8 14.7 %copy-start.7 = (f32[512,384]{1,0:T(8,128)S(1)}, f32[512,384]{1,0:T(8,128)}, u32[]{:S(2)}) copy-start(f32[512,384]{1,0:T(8,128)} %get-tuple-element.32.refs_9_) | copy-start | bytes 2359300
  52.8 14.7 %copy-start.8 = (f32[192,512]{1,0:T(8,128)S(1)}, f32[192,512]{1,0:T(8,128)}, u32[]{:S(2)}) copy-start(f32[192,512]{1,0:T(8,128)} %get-tuple-element.26.refs_2_) | copy-start | bytes 1179652
  52.8 14.7 %copy-start.9 = (bf16[512,384]{1,0:T(8,128)(2,1)S(1)}, bf16[512,384]{1,0:T(8,128)(2,1)}, u32[]{:S(2)}) copy-start(bf16[512,384]{1,0:T(8,128)(2,1)} %get-tuple-element.27.refs_3_) | copy-start | bytes 1179652
  52.8 14.7 %copy-start.10 = (bf16[512,384]{1,0:T(8,128)(2,1)S(1)}, bf16[512,384]{1,0:T(8,128)(2,1)}, u32[]{:S(2)}) copy-start(bf16[512,384]{1,0:T(8,128)(2,1)} %get-tuple-element.33.refs_10_) | copy-start | bytes 1179652
  52.8 14.7 %copy-start.12 = (bf16[192,384]{1,0:T(8,128)(2,1)S(1)}, bf16[192,384]{1,0:T(8,128)(2,1)}, u32[]{:S(2)}) copy-start(bf16[192,384]{1,0:T(8,128)(2,1)} %get-tuple-element.29.refs_6_) | copy-start | bytes 442372
  52.8 14.7 %copy-start.13 = (bf16[512,128]{1,0:T(8,128)(2,1)S(1)}, bf16[512,128]{1,0:T(8,128)(2,1)}, u32[]{:S(2)}) copy-start(bf16[512,128]{1,0:T(8,128)(2,1)} %get-tuple-element.34.refs_12_) | copy-start | bytes 393220
  52.8 59.8 %copy-start.4 = (s32[1,512]{1,0:T(1,128)S(1)}, s32[1,512]{1,0:T(1,128)}, u32[]{:S(2)}) copy-start(s32[1,512]{1,0:T(1,128)} %get-tuple-element.20.refs_0_) | copy-start | bytes 6148
  99.7 24.5 %all-to-all-start.4 = ((f32[16,8,128]{2,1,0:T(8,128)}), f32[16,8,128]{2,1,0:T(8,128)S(1)}, u32[]{:S(2)}, u32[]{:S(2)}) async-start(f32[16,8,128]{2,1,0:T(8,128)} %pieces.1), calls=%async_computation.4 | async-start | bytes 131072 | tf_op jit(solution)/shard_map/all_to_all | solution.py:497

commit v4 on v3

--- a/solution.py
+++ b/solution.py
@@ -22,8 +22,9 @@
 CHUNK = GROUPS + 8
 PIECE = 640
 ALL = 64 * 1024 * 1024
-LIMIT = 48_000_000
+LIMIT = 42_000_000
 PROJECT_LIMIT = 53_500_000
+LOCAL_LIMIT = 54_400_000
 FLOOR = -1e30
 SCALE = 0.125
 LOG_SCALE = 0.125 * math.log2(math.e)
@@ -165,9 +166,9 @@
     code_out,
     far_out,
     fgrad_out,
-    mean_out,
     att_ref,
     dq_ref,
+    mean_out,
     dk_ref,
     dv_ref,
 ):
@@ -227,15 +228,23 @@
     own_bias = jnp.where((iota((1, QUERIES), 1) + first * GROUPS) * STRIDE < last, 0.0, FLOOR)
     key_out = jnp.zeros((QUERIES, 128), F32)
     value_out = jnp.zeros((QUERIES, 128), F32)
-    for i in range(4):
-        rows = slice(i * QUERIES, (i + 1) * QUERIES)
+    def asked(i):
         mine = recv_ref[8 * i : 8 * i + 8, :GROUPS, 128:].reshape(QUERIES, 128)
         query = jnp.where(left, mine, zero)
         grad = jnp.where(left, zero, mine)
         parts = jnp.concatenate([nt(pick, recv_ref[8 * i + j, GROUPS:, :]) for j in range(8)], 0)
+        scores = nt(query, kv) * LOG_SCALE + bias
+        own_scores = nt(query, own_kv) * LOG_SCALE + own_bias
+        return mine, grad, parts, scores, own_scores, nt(grad, own_kv)
+
+    following = asked(0)
+    for i in range(4):
+        rows = slice(i * QUERIES, (i + 1) * QUERIES)
+        mine, grad, parts, scores, own_scores, own_dprob = following
+        if i < 3:
+            following = asked(i + 1)
         lse = parts[:, 0:1] + parts[:, 1:2] + parts[:, 2:3]
         inner = parts[:, 3:4] + parts[:, 4:5] + parts[:, 5:6]
-        scores = nt(query, kv) * LOG_SCALE + bias
         top = jnp.max(scores, -1, keepdims=True)
         weight = jnp.exp2(scores - top)
         ceiling = jnp.maximum(top, lse)
@@ -247,8 +256,8 @@
         numerator = nn(weight.astype(BF), kv) * (gain * inverse)
         stat = jnp.sum(grad.astype(F32) * numerator, -1, keepdims=True) + share * inner
         lse = ceiling + jnp.log2(total)
-        prob = jnp.exp2(nt(query, own_kv) * LOG_SCALE + own_bias - lse)
-        dscore = (prob * (nt(grad, own_kv) - stat) * SCALE).astype(BF)
+        prob = jnp.exp2(own_scores - lse)
+        dscore = (prob * (own_dprob - stat) * SCALE).astype(BF)
         key_out = key_out + tn(dscore, mine)
         value_out = value_out + tn(prob.astype(BF), mine)
         lse_ref[rows] = jnp.broadcast_to(lse, (QUERIES, 128))
@@ -307,26 +316,11 @@
             send_ref[4 * q + r, :, WIDTH:] = pieces[r][16 * q : 16 * q + 16]
 
 
-def finish_kernel(
-    scal_ref,
-    recv_ref,
-    mean_ref,
-    att_ref,
-    cot_ref,
-    far_ref,
-    fgrad_ref,
-    kv_ref,
-    dk_ref,
-    dv_ref,
-    dq_ref,
-    weight_ref,
-    code_ref,
-    send_ref,
-    pair_ref,
-):
+def finish_kernel(scal_ref, recv_ref, held16_ref, held32_ref, cot_ref, weight_ref, send_ref, pair_ref):
+    kv_ref, code_ref, far_ref, fgrad_ref, att_ref, dq_ref = (part(held16_ref, w) for w in HELD16[2])
+    mean_ref, dk_ref, dv_ref = (part(held32_ref, w) for w in HELD32[2])
     share, query_out = returned_far(scal_ref, recv_ref)
     result = far_result(scal_ref, share, query_out, mean_ref[:, :INNER])
-    weight_pieces(result, att_ref, cot_ref, send_ref)
     fq, fgrad = far_ref[...], fgrad_ref[...]
     keys, values = kv_ref[:, :INNER], kv_ref[:, INNER:]
     stat = jnp.sum(fgrad.astype(F32) * result, -1, keepdims=True)
@@ -343,11 +337,11 @@
     far_dk = jnp.where(own, nt(pairs, fold(0)), 0.0).astype(BF)
     far_dv = jnp.where(own, nt(pairs, fold(HD)), 0.0).astype(BF)
     grad_query = dq_ref[...] + tn(chosen, far_dq).astype(BF)
-    grad_key = (dk_ref[...] + tn(dscore, fq) + tn(chosen, far_dk)).astype(BF)
-    grad_value = (dv_ref[...] + tn(prob.astype(BF), fgrad) + tn(chosen, far_dv)).astype(BF)
-    rows = nt(grad_query, weight_ref[:, :INNER])
-    rows = rows + nt(grad_key, weight_ref[:, INNER : 2 * INNER])
-    rows = rows + nt(grad_value, weight_ref[:, 2 * INNER :])
+    grad_key = (dk_ref[...] + tn(jnp.concatenate([dscore, chosen], 0), jnp.concatenate([fq, far_dk], 0))).astype(BF)
+    both = jnp.concatenate([prob.astype(BF), chosen], 0)
+    grad_value = (dv_ref[...] + tn(both, jnp.concatenate([fgrad, far_dv], 0))).astype(BF)
+    weight_pieces(result, att_ref, cot_ref, send_ref)
+    rows = nt(jnp.concatenate([grad_query, grad_key, grad_value], 1), weight_ref[...])
     code = code_ref[...].astype(F32)
     place = (code[:, 0:1] * 16.0 + code[:, 1:2]).astype(jnp.int32)
     order = mark(iota((ROWS, ROWS), 1) == place)
@@ -419,6 +413,17 @@
 MEAN = (0, FAR, 0, INNER + 128)
 LEFT = ((6656, 3 * INNER + 128), BF, (QUERY, KEY_VALUE, CODE, FAR_QUERY, FAR_GRAD))
 GRADS = ((21504, INNER), BF, (QUERY,))
+ATTENTION = (0, ROWS, 3 * INNER + 128, INNER)
+GRAD_QUERY = (0, ROWS, 0, INNER)
+GRAD_KEY = (0, ROWS, 0, INNER)
+GRAD_VALUE = (0, ROWS, INNER, INNER)
+HELD_MEAN = (ROWS, FAR, 0, INNER + 128)
+HELD16 = (
+    (ROWS + FAR, 4 * INNER + 128),
+    BF,
+    (KEY_VALUE, CODE, FAR_QUERY, FAR_GRAD, ATTENTION, GRAD_QUERY),
+)
+HELD32 = ((ROWS + FAR, 2 * INNER), F32, (HELD_MEAN, GRAD_KEY, GRAD_VALUE))
 MEANS = ((8320, INNER + 128), F32, (MEAN,))
 
 
@@ -528,7 +533,7 @@
     )
     far_got = exchange(far_sent, "ctx")
 
-    key_value, code, far_q, far_grad, mean, att, dq, dk, dv, after = call(
+    held16, held32, after = call(
         local_kernel,
         "local_rows",
         12_000_000_000,
@@ -543,18 +548,11 @@
             (means, MEAN),
         ],
         [
-            ((ROWS, 2 * INNER), BF, LATE),
-            ((ROWS, 128), BF, LATE),
-            ((FAR, INNER), BF, LATE),
-            ((FAR, INNER), BF, LATE),
-            ((FAR, INNER + 128), F32, LATE),
-            ((ROWS, INNER), BF, LATE),
-            ((ROWS, INNER), BF, LATE),
-            ((ROWS, INNER), F32, LATE),
-            ((ROWS, INNER), F32, LATE),
+            HELD16,
+            HELD32,
             ((8320, 512), F32, ()),
         ],
-        limit=ALL,
+        limit=LOCAL_LIMIT,
     )
 
     (far_back,) = call(
@@ -577,17 +575,10 @@
         [
             (lengths, SCALAR),
             (far_back, HERE),
-            (mean, HERE),
-            (att, HERE),
+            (held16, HERE),
+            (held32, HERE),
             (cot, HERE),
-            (far_q, HERE),
-            (far_grad, HERE),
-            (key_value, HERE),
-            (dk, HERE),
-            (dv, HERE),
-            (dq, HERE),
             (qkv_weight, HERE),
-            (code, HERE),
         ],
         [((PEERS, PORTION, WIDTH + PIECE), BF, HERE), ((2, FAR, HD), F32, LATE)],
     )

time: 125 us -> 123 us (0.984)
  Pallas kernels: 33.4 us -> 31.4 us
    pallas_call x8, Pallas kernels: 33.4 us -> 31.4 us  [call(): pl.pallas_call(kernel, out_shape=[jax.ShapeDtypeStruct(dims, dtype) for d...]
  transfers between devices with their start and end apart: 3 -> 3, of which waited for: 3 -> 3; matrix products, arithmetic and copies ran while one was open for 0% -> 0% of each run, Pallas kernels for 10% -> 11%
where the time goes in v4:
time: 123 us; the launch traced here: 122 us
  blocking collectives  34.4 us (28%)
  Pallas kernels  31.4 us (26%)
  starting transfers between devices  27.5 us (22%)
  waiting for transfers between devices  25.7 us (21%)
  between operations  1.4 us (1%)
    pallas_call x8, Pallas kernels, call(): pl.pallas_call(kernel, out_shape=[jax.ShapeDtypeStruct(dims, dtype) for d...  31.4 us
    all_to_all x3, starting transfers between devices, exchange(): return lax.all_to_all(rows, axis, split_axis=0, concat_axis=0, tiled=True)  27.5 us
    all_to_all x1, blocking collectives, exchange(): return lax.all_to_all(rows, axis, split_axis=0, concat_axis=0, tiled=True)  25.8 us
    all_to_all x3, waiting for transfers between devices, exchange(): return lax.all_to_all(rows, axis, split_axis=0, concat_axis=0, tiled=True)  25.7 us
    all_to_all x1, blocking collectives, local(): lax.all_to_all(far_back, 'ctx', split_axis=0, concat_axis=0, axis_index_g...  8.52 us
  transfers between devices with their start and end apart: 3, of which 3 were waited for; matrix products, arithmetic and copies ran while one was open for 0% of the time, Pallas kernels for 11%

profile of v4, /device:TPU:1, one launch (start us, length us, event | category | flops | bytes accessed | tf_op | source)
XLA Modules:
  0.0 122.1 jit_solution(4390232906735654684)
XLA Ops:
  0.6 2.8 %pack.1 = (bf16[512,896]{1,0:T(8,128)(2,1)}, s32[1,512]{1,0:T(1,128)}) custom-call(s32[1,512]{1,0:T(1,128)} %refs_0_.7, bf16[512,768]{1,0:T(8,128)(2,1)} %bitcast.14), custom_call_target="tpu_custom_call" | custom-call | flops 800000000 | bytes 4000000 | tf_op jit(solution)/shard_map/pack/pallas_call | solution.py:487
  3.5 0.0 copy-start.1
  3.5 10.6 %all-to-all-start = ((bf16[32,16,896]{2,1,0:T(8,128)(2,1)}), bf16[32,16,896]{2,1,0:T(8,128)(2,1)S(1)}, u32[]{:S(2)}, u32[]{:S(2)}) async-start(bf16[32,16,896]{2,1,0:T(8,128)(2,1)} %bitcast.11), calls=%async_computation | async-start | bytes 1835008 | tf_op jit(solution)/shard_map/all_to_all | solution.py:502
  14.7 0.0 copy-done.1
  14.7 0.0 copy-start.2
  14.7 1.1 copy-done.2
  15.8 1.6 %grad.1.refs_3_ = bf16[21504,384]{1,0:T(8,128)(2,1)} custom-call(s32[1]{0:T(128)S(6)} %copy.9.refs_0_, bf16[512,768]{1,0:T(8,128)(2,1)S(1)} %bitcast.9, bf16[384,768]{1,0:T(8,128)(2,1)S(1)} %copy-done.2), custom_call_target="tpu_custom_call" | custom-call | flops 400000000 | bytes 4000000 | tf_op jit(solution)/shard_map/grad/pallas_call | solution.py:487
  17.4 12.6 %all-to-all-done = bf16[32,16,896]{2,1,0:T(8,128)(2,1)S(1)} async-done(((bf16[32,16,896]{2,1,0:T(8,128)(2,1)}), bf16[32,16,896]{2,1,0:T(8,128)(2,1)S(1)}, u32[]{:S(2)}, u32[]{:S(2)}) %all-to-all-start) | async-done | bytes 917536 | tf_op jit(solution)/shard_map/all_to_all | solution.py:502
  30.0 5.2 %project.1 = (bf16[32,40,256]{2,1,0:T(8,128)(2,1)}, bf16[6656,1280]{1,0:T(8,128)(2,1)}, f32[8320,512]{1,0:T(8,128)}) custom-call(s32[1]{0:T(128)S(6)} %copy.9.refs_0_, bf16[512,896]{1,0:T(8,128)(2,1)S(1)} %bitcast.8, bf16[768,1152]{1,0:T(8,128)(2,1)} %refs_5_.1, bf16[21504,384]{1,0:T(8,128)(2,1)} %grad.1.refs_3_), custom_call_target="tpu_custom_call" | custom-call | flops 3000000000 | bytes 4000000 | tf_op jit(solution)/shard_map/project/pallas_call | solution.py:487
  35.1 4.0 %all-to-all-start.1 = ((bf16[32,40,256]{2,1,0:T(8,128)(2,1)}), bf16[32,40,256]{2,1,0:T(8,128)(2,1)S(1)}, u32[]{:S(2)}, u32[]{:S(2)}) async-start(bf16[32,40,256]{2,1,0:T(8,128)(2,1)} %get-tuple-element.15), calls=%async_computation.1 | async-start | bytes 1310720 | tf_op jit(solution)/shard_map/all_to_all | solution.py:502
  39.1 9.8 %local_rows.1 = (bf16[704,1664]{1,0:T(8,128)(2,1)}, f32[704,768]{1,0:T(8,128)}, f32[8320,512]{1,0:T(8,128)}) custom-call(s32[1]{0:T(128)S(6)} %copy.9.refs_0_, bf16[6656,1280]{1,0:T(8,128)(2,1)} %get-tuple-element.16.refs_1_.refs_2_.refs_4_.refs_5_.refs_6_, bf16[6656,1280]{1,0:T(8,128)(2,1)} %get-tuple-element.16.refs_1_.refs_2_.refs_4_.refs_5_.refs_6_, ...), custom_call_target="tpu_custom_call" | custom-call | flops 12000000000 | bytes 4000000 | tf_op jit(solution)/shard_map/local_rows/pallas_call | solution.py:487
  49.0 3.2 %all-to-all-done.1.refs_1_ = bf16[32,40,256]{2,1,0:T(8,128)(2,1)S(1)} async-done(((bf16[32,40,256]{2,1,0:T(8,128)(2,1)}), bf16[32,40,256]{2,1,0:T(8,128)(2,1)S(1)}, u32[]{:S(2)}, u32[]{:S(2)}) %all-to-all-start.1) | async-done | bytes 655392 | tf_op jit(solution)/shard_map/all_to_all | solution.py:502
  52.1 0.0 copy-start
  52.1 0.0 copy-start.4
  52.1 0.0 copy-start.5
  52.1 5.0 %far.1 = bf16[8,40,256]{2,1,0:T(8,128)(2,1)S(1)} custom-call(s32[1]{0:T(128)S(6)} %copy.9.refs_0_, bf16[32,40,256]{2,1,0:T(8,128)(2,1)S(1)} %all-to-all-done.1.refs_1_, f32[8320,512]{1,0:T(8,128)} %get-tuple-element.18.refs_2_), custom_call_target="tpu_custom_call" | custom-call | flops 6000000000 | bytes 4000000 | tf_op jit(solution)/shard_map/far/pallas_call | solution.py:487
  57.1 8.5 %all_to_all.25.refs_1_ = bf16[8,40,256]{2,1,0:T(8,128)(2,1)S(1)} all-to-all(bf16[8,40,256]{2,1,0:T(8,128)(2,1)S(1)} %far.1), channel_id=1, replica_groups={{0,1,2,3,4,5,6,7},{8,9,10,11,12,13,14,15},{16,17,18,19,20,21,22,23},{24..., dimensions={0} | all-to-all | bytes 327680 | tf_op jit(solution)/shard_map/all_to_all | solution.py:567
  65.6 0.0 copy-done
  65.6 0.0 copy-done.4
  65.6 0.0 copy-done.5
  65.6 4.6 %finish.1 = (bf16[32,16,1408]{2,1,0:T(8,128)(2,1)S(1)}, f32[2,192,64]{2,1,0:T(8,128)}) custom-call(s32[1]{0:T(128)S(6)} %copy.9.refs_0_, bf16[8,40,256]{2,1,0:T(8,128)(2,1)S(1)} %all_to_all.25.refs_1_, bf16[704,1664]{1,0:T(8,128)(2,1)S(1)} %copy-done.4, f32[704,768]{1,0:T(8,128)S(1)} %copy-done.5, bf16[512,768]{1,0:T(8,128)(2,1)S(1)} %bitcast.10, ...), custom_call_target="tpu_custom_call" | custom-call | flops 4000000000 | bytes 4000000 | tf_op jit(solution)/shard_map/finish/pallas_call | solution.py:487
  70.3 0.0 copy-start.3
  70.3 25.8 %all_to_all.26.refs_1_ = bf16[32,16,1408]{2,1,0:T(8,128)(2,1)S(1)} all-to-all(bf16[32,16,1408]{2,1,0:T(8,128)(2,1)S(1)} %get-tuple-element.21), channel_id=1, replica_groups=mesh['slide'=16,'ctx'=32] {'ctx'}, dimensions={0} | all-to-all | bytes 2883584 | tf_op jit(solution)/shard_map/all_to_all | solution.py:502
  96.1 0.8 pieces.1
  96.9 13.0 %all-to-all-start.4 = ((f32[16,8,128]{2,1,0:T(8,128)}), f32[16,8,128]{2,1,0:T(8,128)S(1)}, u32[]{:S(2)}, u32[]{:S(2)}) async-start(f32[16,8,128]{2,1,0:T(8,128)} %pieces.1), calls=%async_computation.4 | async-start | bytes 131072 | tf_op jit(solution)/shard_map/all_to_all | solution.py:502
  109.9 0.0 copy-done.3
  109.9 1.5 %unpack.1 = bf16[512,768]{1,0:T(8,128)(2,1)} custom-call(s32[1,512]{1,0:T(1,128)S(1)} %copy-done.3, bf16[32,16,1408]{2,1,0:T(8,128)(2,1)S(1)} %all_to_all.26.refs_1_), custom_call_target="tpu_custom_call" | custom-call | flops 400000000 | bytes 4000000 | tf_op jit(solution)/shard_map/unpack/pallas_call | solution.py:487
  111.5 10.0 %all-to-all-done.4 = f32[16,8,128]{2,1,0:T(8,128)S(1)} async-done(((f32[16,8,128]{2,1,0:T(8,128)}), f32[16,8,128]{2,1,0:T(8,128)S(1)}, u32[]{:S(2)}, u32[]{:S(2)}) %all-to-all-start.4) | async-done | bytes 65568 | tf_op jit(solution)/shard_map/all_to_all | solution.py:502
  121.5 0.6 reduce_sum.9
Async XLA Ops:
  3.5 11.3 %copy-start.1 = (bf16[1,512,768]{2,1,0:T(8,128)(2,1)S(1)}, bf16[1,512,768]{2,1,0:T(8,128)(2,1)}, u32[]{:S(2)}) copy-start(bf16[1,512,768]{2,1,0:T(8,128)(2,1)} %param.11) | copy-start | bytes 2359300
  3.5 26.5 %all-to-all-start = ((bf16[32,16,896]{2,1,0:T(8,128)(2,1)}), bf16[32,16,896]{2,1,0:T(8,128)(2,1)S(1)}, u32[]{:S(2)}, u32[]{:S(2)}) async-start(bf16[32,16,896]{2,1,0:T(8,128)(2,1)} %bitcast.11), calls=%async_computation | async-start | bytes 1835008 | tf_op jit(solution)/shard_map/all_to_all | solution.py:502
  14.7 1.1 copy-start.2
  35.1 17.0 %all-to-all-start.1 = ((bf16[32,40,256]{2,1,0:T(8,128)(2,1)}), bf16[32,40,256]{2,1,0:T(8,128)(2,1)S(1)}, u32[]{:S(2)}, u32[]{:S(2)}) async-start(bf16[32,40,256]{2,1,0:T(8,128)(2,1)} %get-tuple-element.15), calls=%async_computation.1 | async-start | bytes 1310720 | tf_op jit(solution)/shard_map/all_to_all | solution.py:502
  52.1 13.5 %copy-start = (bf16[768,1152]{1,0:T(8,128)(2,1)S(1)}, bf16[768,1152]{1,0:T(8,128)(2,1)}, u32[]{:S(2)}) copy-start(bf16[768,1152]{1,0:T(8,128)(2,1)} %refs_5_.1) | copy-start | bytes 5308420
  52.1 13.5 %copy-start.4 = (bf16[704,1664]{1,0:T(8,128)(2,1)S(1)}, bf16[704,1664]{1,0:T(8,128)(2,1)}, u32[]{:S(2)}) copy-start(bf16[704,1664]{1,0:T(8,128)(2,1)} %get-tuple-element.19.refs_2_) | copy-start | bytes 7028740
  52.1 13.5 %copy-start.5 = (f32[704,768]{1,0:T(8,128)S(1)}, f32[704,768]{1,0:T(8,128)}, u32[]{:S(2)}) copy-start(f32[704,768]{1,0:T(8,128)} %get-tuple-element.20.refs_3_) | copy-start | bytes 6488068
  70.3 39.6 %copy-start.3 = (s32[1,512]{1,0:T(1,128)S(1)}, s32[1,512]{1,0:T(1,128)}, u32[]{:S(2)}) copy-start(s32[1,512]{1,0:T(1,128)} %get-tuple-element.13.refs_0_) | copy-start | bytes 6148
  96.9 24.6 %all-to-all-start.4 = ((f32[16,8,128]{2,1,0:T(8,128)}), f32[16,8,128]{2,1,0:T(8,128)S(1)}, u32[]{:S(2)}, u32[]{:S(2)}) async-start(f32[16,8,128]{2,1,0:T(8,128)} %pieces.1), calls=%async_computation.4 | async-start | bytes 131072 | tf_op jit(solution)/shard_map/all_to_all | solution.py:502
